TPU v7x, 32 devices: a whole 2x2x4 slice. The times are simulated.
32 devices in a mesh: pair: 4 (over z), tm: 8 (over y, x, core).
Axes of the slice: x: 2, y: 2, z: 4, core: 2. Of those that a mesh axis runs over, the one named last changes fastest.
Arguments:
- records: bfloat16 [256, 128, 2048], P('pair', 'tm'), may hold values from -60 to 60, as said below
- pair_list: int32 [512, 2], replicated, may hold values from 0 to 255, as said below
- sketch: float32 [16, 2048], replicated, may hold values from -6 to 6
Outputs:
- stacks: float32 [512, 2048], P('pair')
Inputs may be any that keep to these rules, and one draw needn't show every extreme that they name: `pair_list`: rows p * 128 to (p + 1) * 128 - 1 name at most 12 distinct channels from any one block of channels o * 64 to (o + 1) * 64 - 1, and exactly 12 from one such block; the 128 channel slots of a pair index cycle through its listed channels, so each listed channel is used. `records`: each channel is a delayed copy of a field common to all channels plus its own noise, times a channel gain.
All inputs are finite; a program needn't handle non-finite values.
Results may differ from a plain program's by a relative error of at most 0.0041.
The roundings to bfloat16 on the way count: a program that leaves them out, or rounds other values in their place, can miss the bound.
Values may be sent and summed in bfloat16 or wider, within the bound.
A program may use at most 192 MiB of HBM per device.

v0:
```python
import math

import jax
import jax.numpy as jnp
from jax import lax
from jax.sharding import PartitionSpec as P

SAMPLES = 2048
NF = 512
LAGS = 2048
CAP = 12
PAIRS_DEV = 128


def tables():
    freq = NF // 2 + jnp.arange(NF)
    times = jnp.arange(SAMPLES)
    turn = jnp.mod(times[:, None] * freq[None, :], SAMPLES).astype(jnp.float32) * (
        2.0 * math.pi / SAMPLES
    )
    forward = jnp.concatenate([jnp.cos(turn), jnp.sin(turn)], axis=1).astype(jnp.bfloat16)
    shifts = jnp.arange(LAGS) - LAGS // 2
    angle = jnp.mod(freq[:, None] * shifts[None, :], SAMPLES).astype(jnp.float32) * (
        2.0 * math.pi / SAMPLES
    )
    inverse = (jnp.concatenate([jnp.cos(angle), -jnp.sin(angle)], axis=0) / math.sqrt(NF)).astype(
        jnp.bfloat16
    )
    return (forward, inverse)


def whiten(block, forward):
    spectra = jnp.dot(block, forward, preferred_element_type=jnp.float32)
    real_part = spectra[:, :NF]
    imag_part = spectra[:, NF:]
    power = real_part * real_part + imag_part * imag_part
    level = jnp.mean(power, axis=1, keepdims=True)
    factor = lax.rsqrt(power + level + 1e-06)
    return jnp.concatenate([real_part * factor, imag_part * factor], axis=1).astype(jnp.bfloat16)


def correlate(first, second):
    left = first.astype(jnp.float32)
    right = second.astype(jnp.float32)
    lre, lim = (left[..., :NF], left[..., NF:])
    rre, rim = (right[..., :NF], right[..., NF:])
    return jnp.concatenate([lre * rre + lim * rim, lim * rre - lre * rim], axis=-1).astype(
        jnp.bfloat16
    )


def orthonormal(raw):
    highest = lax.Precision.HIGHEST
    gram = jnp.einsum("prl,psl->prs", raw, raw, precision=highest)
    lower = jnp.linalg.cholesky(gram)
    return lax.linalg.triangular_solve(lower, raw, left_side=True, lower=True)


def local(records, pair_list, sketch):
    highest = lax.Precision.HIGHEST
    forward, inverse = tables()
    n_pair = lax.axis_size("pair")
    owner = lax.axis_index("pair")
    ch_dev, win_dev, samples = records.shape
    white = whiten(records.reshape(ch_dev * win_dev, samples), forward).reshape(
        ch_dev, win_dev, 2 * NF
    )
    mine = lax.dynamic_slice_in_dim(pair_list, owner * PAIRS_DEV, PAIRS_DEV, 0)
    wanted = pair_list.reshape(n_pair, 2 * PAIRS_DEV) - owner * ch_dev
    column = jnp.arange(ch_dev)
    asked = jnp.any(wanted[:, None, :] == column[None, :, None], axis=2)
    order = jnp.cumsum(asked.astype(jnp.int32), axis=1) - 1
    slots = jnp.arange(CAP)
    picker = (asked[:, None, :] & (order[:, None, :] == slots[None, :, None])).astype(jnp.bfloat16)
    outgoing = jnp.einsum(
        "dkc,cwf->dkwf", picker, white, preferred_element_type=jnp.float32
    ).astype(jnp.bfloat16)
    everyone = jnp.arange(n_pair * ch_dev)
    held = jnp.any(mine.reshape(-1)[None, :] == everyone[:, None], axis=1).reshape(n_pair, ch_dev)
    rank_of = (jnp.cumsum(held.astype(jnp.int32), axis=1) - 1).reshape(-1)
    first_slot = mine[:, 0] // ch_dev * CAP + jnp.take(rank_of, mine[:, 0])
    second_slot = mine[:, 1] // ch_dev * CAP + jnp.take(rank_of, mine[:, 1])
    arrived = lax.all_to_all(outgoing, "pair", split_axis=0, concat_axis=0, tiled=True)
    flat = arrived.reshape(n_pair * CAP, arrived.shape[2], arrived.shape[3])
    cross = correlate(jnp.take(flat, first_slot, axis=0), jnp.take(flat, second_slot, axis=0))
    crossf = cross.astype(jnp.float32)
    energy_local = jnp.sum(crossf * crossf, axis=(1, 2))
    lagged = jnp.einsum("pwf,fl->pwl", cross, inverse, preferred_element_type=jnp.float32)
    probe = jnp.einsum("pwl,rl->pwr", lagged, sketch, precision=highest)
    partial_raw = jnp.einsum("pwr,pwl->prl", probe, lagged, precision=highest)
    raw, energy = lax.psum((partial_raw, energy_local), "tm")
    basis = orthonormal(raw)
    coeffs = jnp.einsum("pwl,prl->pwr", lagged, basis, precision=highest)
    total, power = lax.psum((jnp.sum(coeffs, axis=1), jnp.sum(coeffs * coeffs, axis=1)), "tm")
    gain = power / (power + energy[:, None] / (2 * NF))
    windows = win_dev * lax.axis_size("tm")
    return jnp.einsum("pr,prl->pl", gain * total / windows, basis, precision=highest)


def solution(mesh):
    in_specs = (P("pair", "tm", None), P(), P())
    out_specs = P("pair", None)
    return jax.shard_map(local, mesh=mesh, in_specs=in_specs, out_specs=out_specs, check_vma=False)
```

profile of v0, /device:TPU:9, one launch (start us, length us, event | category | flops | bytes accessed | tf_op | source)
XLA Modules:
  0.0 695.3 jit_solution(16730171264493113726)
XLA Ops:
  6.5 0.7 broadcast_subtract_fusion
  8.0 16.8 %cosine_convert_fusion = (bf16[2048,512]{1,0:T(8,128)(2,1)S(1)}, bf16[2048,512]{1,0:T(8,128)(2,1)S(1)}) fusion(s32[512]{0:T(512)S(1)} %iota_add_fusion.1), kind=kLoop, calls=%fused_computation.41 | loop fusion | flops 16777216 | bytes 4196352 | tf_op jit(solution)/shard_map/convert.7
  24.9 4.5 fusion.24
  29.7 0.7 multiply_convert_fusion.1
  30.4 0.6 copy.41
  31.0 0.6 copy.42
  31.6 0.7 fusion.31
  32.3 2.0 copy.43
  34.3 4.8 all-to-all-start
  39.1 0.7 constant_dynamic-slice_fusion
  40.6 1.3 gather_fusion.2
  41.8 1.3 gather_fusion
  43.2 19.4 %fusion.30 = (f32[512,2048]{1,0:T(8,128)}, f32[512,2048]{1,0:T(8,128)}) fusion(s32[2048]{0:T(1024)S(1)} %iota_add_fusion, s32[512]{0:T(512)S(1)} %iota_add_fusion.1), kind=kLoop, calls=%fused_computation.50 | loop fusion | flops 15728640 | bytes 8398848 | tf_op jit(solution)/shard_map/cos | solution.py:26
  62.6 9.5 %all-to-all-done = bf16[4,12,16,1024]{3,2,1,0:T(8,128)(2,1)S(1)} async-done(((bf16[4,12,16,1024]{3,2,1,0:T(8,128)(2,1)}), bf16[4,12,16,1024]{3,2,1,0:T(8,128)(2,1)S(1)}, u32[]{:S(2)}, u32[]{:S(2)}) %all-to-all-start) | async-done | bytes 1572896 | tf_op jit(solution)/shard_map/all_to_all | solution.py:83
  72.1 2.8 gather_fusion.3
  74.9 2.8 gather_fusion.1
  77.7 7.2 %fusion.19 = f32[128,16,1024]{2,0,1:T(8,128)S(1)} fusion(bf16[128,16,1024]{2,1,0:T(8,128)(2,1)} %gather_fusion.1, pred[128]{0:T(512)(128)(4,1)S(1)} %get-tuple-element.12), kind=kLoop, calls=%fused_computation.35 | loop fusion | flops 4194304 | bytes 12583040 | tf_op jit(solution)/shard_map/convert_element_type | solution.py:43
  84.9 4.9 fusion.18
  89.8 2.6 add_convert_fusion
  92.4 14.6 %fusion.12 = f32[128,16,2048]{2,0,1:T(8,128)} fusion(f32[512,2048]{1,0:T(8,128)} %get-tuple-element.21, f32[512,2048]{1,0:T(8,128)S(1)} %copy-done.4, bf16[128,16,512]{2,0,1:T(8,128)(2,1)S(1)} %get-tuple-element.17, bf16[128,16,512]{2,0,1:T(8,128)(2,1)S(1)} %get-tuple-element.16), kind=kOutput, calls=%fused_computation.26 | convolution fusion | flops 8604614656 | bytes 29360128 | tf_op jit(solution)/shard_map/pwf,fl->pwl/dot_general | solution.py:88
  107.1 16.6 %fusion.35 = f32[128,16,16]{0,2,1:T(8,128)S(1)} fusion(f32[128,16,2048]{2,0,1:T(8,128)} %fusion.12, f32[16,2048]{1,0:T(8,128)S(1)} %copy-done), kind=kOutput, calls=%fused_computation.64 | convolution fusion | flops 805306368 | bytes 17039360 | tf_op jit(solution)/shard_map/pwl,rl->pwr/dot_general | solution.py:89
  124.2 32.3 %fusion = f32[128,16,2048]{2,1,0:T(8,128)} fusion(f32[128,16,16]{1,2,0:T(8,128)S(1)} %copy.46, f32[128,16,2048]{2,0,1:T(8,128)} %fusion.12), kind=kOutput, calls=%fused_computation.4 | convolution fusion | flops 805306368 | bytes 33685504 | tf_op jit(solution)/shard_map/pwr,pwl->prl/dot_general | solution.py:90
  156.6 2.2 multiply_reduce_fusion
  158.8 219.0 %all-reduce.3.cloned.1.call-done = f32[128,16,2048]{2,1,0:T(8,128)} async-done(((f32[128,16,2048]{2,1,0:T(8,128)}), f32[128,16,2048]{2,1,0:T(8,128)}) %all-reduce.3.cloned.1.call-update) | async-done | bytes 16777232 | tf_op jit(solution)/shard_map/psum | solution.py:91
  377.9 25.8 %fusion.52 = f32[128,16,16]{2,1,0:T(8,128)S(1)} fusion(f32[128,16,2048]{2,1,0:T(8,128)} %all-reduce.3.cloned.1.call-done), kind=kOutput, calls=%fused_computation.117 | convolution fusion | flops 805306368 | bytes 16908288 | tf_op jit(solution)/shard_map/prl,psl->prs/dot_general | solution.py:54
  404.2 187.6 %custom-call.7 = f32[128,16,16]{2,1,0:T(8,128)S(1)} custom-call(f32[128,16,16]{2,1,0:T(8,128)S(1)} %fusion.32), custom_call_target="Cholesky" | custom-call | tf_op jit(solution)/shard_map/jit(cholesky)/cholesky | solution.py:55
  592.4 2.7 custom-call.8
  595.7 21.5 %fusion.53 = f32[128,16,2048]{2,1,0:T(8,128)} fusion(f32[128,16,16]{2,1,0:T(8,128)S(1)} %copy.51, f32[128,16,2048]{2,1,0:T(8,128)} %all-reduce.3.cloned.1.call-done), kind=kOutput, calls=%fused_computation.118 | convolution fusion | flops 805306368 | bytes 33685504 | tf_op jit(solution)/shard_map/triangular_solve | solution.py:56
  617.1 35.2 %multiply_reduce_fusion.1 = (f32[128,16]{1,0:T(8,128)S(1)}, f32[128,16]{1,0:T(8,128)S(1)}) fusion(f32[128,16,2048]{2,1,0:T(8,128)} %fusion.53, f32[128,16,2048]{2,0,1:T(8,128)} %fusion.12), kind=kOutput, calls=%fused_computation.59 | convolution fusion | flops 805400576 | bytes 33570816 | tf_op jit(solution)/shard_map/pwl,prl->pwr/dot_general | solution.py:93
  652.4 22.9 %all-reduce = (f32[128,16]{1,0:T(8,128)S(1)}, f32[128,16]{1,0:T(8,128)S(1)}, f32[128]{0:T(128)S(1)}) all-reduce(f32[128,16]{1,0:T(8,128)S(1)} %get-tuple-element.8, f32[128,16]{1,0:T(8,128)S(1)} %get-tuple-element.6, f32[128]{0:T(128)S(1)} %multiply_reduce_fusion), channel_id=1, replica_groups=mesh['pair'=4,'tm'=8] {'tm'}, use_global_device_ids=true, to_apply=%region_13.16 | all-reduce | flops 4224 | bytes 33792 | tf_op jit(solution)/shard_map/psum | solution.py:94
  675.4 11.5 %fusion.54 = f32[128,1,2048]{2,1,0:T(1,128)S(1)} fusion(f32[128,16,1]{1,2,0:T(1,128)S(1)} %bitcast.81, f32[128,16,2048]{2,1,0:T(8,128)} %fusion.53), kind=kOutput, calls=%fused_computation.119 | convolution fusion | flops 50331648 | bytes 17833984 | tf_op jit(solution)/shard_map/pr,prl->pl/dot_general | solution.py:97
  686.9 1.3 copy.69
  (49 shorter events, 4.2 us)
Async XLA Ops:
  6.5 100.5 %copy-start = (f32[16,2048]{1,0:T(8,128)S(1)}, f32[16,2048]{1,0:T(8,128)}, u32[]{:S(2)}) copy-start(f32[16,2048]{1,0:T(8,128)} %param.9) | copy-start | bytes 393220
  8.0 16.8 %copy-start.5 = (bf16[64,16,2048]{2,1,0:T(8,128)(2,1)S(1)}, bf16[64,16,2048]{2,1,0:T(8,128)(2,1)}, u32[]{:S(2)}) copy-start(bf16[64,16,2048]{2,1,0:T(8,128)(2,1)} %param.7) | copy-start | bytes 12582916
  34.3 37.8 %all-to-all-start = ((bf16[4,12,16,1024]{3,2,1,0:T(8,128)(2,1)}), bf16[4,12,16,1024]{3,2,1,0:T(8,128)(2,1)S(1)}, u32[]{:S(2)}, u32[]{:S(2)}) async-start(bf16[4,12,16,1024]{3,2,1,0:T(8,128)(2,1)} %copy.43), calls=%async_computation | async-start | bytes 3145728 | tf_op jit(solution)/shard_map/all_to_all | solution.py:83
  39.0 338.8 %all-reduce.3.cloned.1.call-start = ((), (), s32[]{:S(2)}) async-start(), calls=%async_computation.1 | async-start | bytes 33554432 | tf_op jit(solution)/shard_map/psum | solution.py:91
  77.7 7.2 %copy-start.2 = (bf16[128,16,1024]{2,1,0:T(8,128)(2,1)S(1)}, bf16[128,16,1024]{2,1,0:T(8,128)(2,1)}, u32[]{:S(2)}) copy-start(bf16[128,16,1024]{2,1,0:T(8,128)(2,1)} %gather_fusion.3) | copy-start | bytes 12582916
  89.7 2.7 copy-start.4
  92.4 14.7 %copy-start.3 = (bf16[128,16,512]{2,0,1:T(8,128)(2,1)}, bf16[128,16,512]{2,0,1:T(8,128)(2,1)S(1)}, u32[]{:S(2)}) copy-start(bf16[128,16,512]{2,0,1:T(8,128)(2,1)S(1)} %get-tuple-element.17) | copy-start | bytes 6291460
  675.4 12.9 %copy-start.1 = (f32[16,2048]{1,0:T(8,128)S(1)}, f32[16,2048]{1,0:T(8,128)}, u32[]{:S(2)}) copy-start(f32[16,2048]{1,0:T(8,128)} %param.9) | copy-start | bytes 393220
Sparse Core Ops, SparseCore 0:
  156.7 221.1 all-reduce.2
where the time goes:
time: 708 us; the launch traced here: 695 us
  other arithmetic  247 us (35%)
  waiting for transfers between devices  229 us (32%)
  matrix products  163 us (23%)
  blocking collectives  22.9 us (3%)
  local copies, waits for them, and re-layouts  15.8 us (2%)
  between operations  13.9 us (2%)
    psum x1, waiting for transfers between devices, local(): raw, energy = lax.psum((partial_raw, energy_local), 'tm')  219 us
    another operation x4, other arithmetic, orthonormal(): lower = jnp.linalg.cholesky(gram)  188 us
    dot_general x1, matrix products, local(): coeffs = jnp.einsum('pwl,prl->pwr', lagged, basis, precision=highest)  35.2 us
    dot_general x1, matrix products, local(): partial_raw = jnp.einsum('pwr,pwl->prl', probe, lagged, precision=highest)  32.3 us
    dot_general x1, matrix products, orthonormal(): gram = jnp.einsum('prl,psl->prs', raw, raw, precision=highest)  25.8 us
    psum x1, blocking collectives, local(): lax.psum((jnp.sum(coeffs, axis=1), jnp.sum(coeffs * coeffs, axis=1)), 'tm')  22.9 us
    another operation x1, matrix products, orthonormal(): return lax.linalg.triangular_solve(lower, raw, left_side=True, lower=True)  21.5 us
    another operation x3, other arithmetic  20.1 us
  transfers between devices with their start and end apart: 2, of which 2 were waited for; matrix products, arithmetic and copies ran while one was open for 4% of the time, Pallas kernels for 0%

commit v1 on v0

v1 whole, which is shorter than its diff:
```python
import functools
import math

import jax
import jax.numpy as jnp
import numpy as np
from jax import lax
from jax.experimental import pallas as pl
from jax.experimental.pallas import tpu as pltpu
from jax.sharding import Mesh
from jax.sharding import PartitionSpec as P

SAMPLES = 2048
NF = 512
LAGS = 2048
RANK = 16
CAP = 12
PAIRS_DEV = 128
GROUP = 8
BF = jnp.bfloat16
F32 = jnp.float32
HIGHEST = lax.Precision.HIGHEST
VMEM = 56 * 1024 * 1024
NT = (((1,), (1,)), ((), ()))


def tables():
    freq = NF // 2 + np.arange(NF)
    scale = np.float32(2.0 * math.pi / SAMPLES)
    times = np.arange(SAMPLES)
    turn = np.mod(times[:, None] * freq[None, :], SAMPLES).astype(np.float32) * scale
    forward = np.concatenate([np.cos(turn), np.sin(turn)], axis=1).astype(jnp.bfloat16)
    shifts = np.arange(LAGS) - LAGS // 2
    angle = np.mod(freq[:, None] * shifts[None, :], SAMPLES).astype(np.float32) * scale
    inverse = (
        np.concatenate([np.cos(angle), -np.sin(angle)], axis=0) / np.float32(math.sqrt(NF))
    ).astype(jnp.bfloat16)
    wide = inverse.astype(np.float64)
    return forward, inverse, (wide @ wide.T).astype(np.float32)


def split(x):
    high = x.astype(BF)
    return high, (x - high.astype(F32)).astype(BF)


def dot(a, b, dims=(((1,), (0,)), ((), ()))):
    return lax.dot_general(a, b, dims, preferred_element_type=F32)


def params():
    return pltpu.CompilerParams(vmem_limit_bytes=VMEM)


def white_kernel(idx_ref, *refs):
    blocks, forward_ref, out_ref = refs[:CAP], refs[CAP], refs[CAP + 1]
    block = jnp.concatenate([b[0] for b in blocks], axis=0)
    spectra = dot(block, forward_ref[...])
    re, im = spectra[:, :NF], spectra[:, NF:]
    power = re * re + im * im
    level = jnp.mean(power, axis=1, keepdims=True)
    factor = lax.rsqrt(power + level + 1e-06)
    rows = block.shape[0] // CAP
    out_ref[0, :, :, :NF] = (re * factor).astype(BF).reshape(CAP, rows, NF)
    out_ref[0, :, :, NF:] = (im * factor).astype(BF).reshape(CAP, rows, NF)


def whiten(records, idx, forward):
    _, win, samples = records.shape
    n = idx.shape[0] // CAP

    def pick(k):
        return pl.BlockSpec((1, win, samples), lambda d, idx, k=k: (idx[d * CAP + k], 0, 0))

    return pl.pallas_call(
        white_kernel,
        grid_spec=pltpu.PrefetchScalarGridSpec(
            num_scalar_prefetch=1,
            grid=(n,),
            in_specs=[pick(k) for k in range(CAP)]
            + [pl.BlockSpec(forward.shape, lambda d, idx: (0, 0))],
            out_specs=pl.BlockSpec((1, CAP, win, 2 * NF), lambda d, idx: (d, 0, 0, 0)),
        ),
        out_shape=jax.ShapeDtypeStruct((n, CAP, win, 2 * NF), BF),
        compiler_params=params(),
        name="whiten",
    )(idx, *([records] * CAP), forward)


def own_block(rows, row_size, cols, col_size):
    r = lax.broadcasted_iota(jnp.int32, (rows, cols), 0) // row_size
    c = lax.broadcasted_iota(jnp.int32, (rows, cols), 1) // col_size
    return r == c


def cross_kernel(slot_ref, flat_ref, high_ref, low_ref, cross_ref, raw_ref):
    step = pl.program_id(0)
    parts, _, win, _ = flat_ref.shape
    for q in range(GROUP):
        a = slot_ref[(step * GROUP + q) * 2]
        b = slot_ref[(step * GROUP + q) * 2 + 1]
        for part in range(parts):
            left = flat_ref[part, a].astype(F32)
            right = flat_ref[part, b].astype(F32)
            lre, lim = left[:, :NF], left[:, NF:]
            rre, rim = right[:, :NF], right[:, NF:]
            rows = pl.ds((q * parts + part) * win, win)
            cross_ref[rows, :NF] = (lre * rre + lim * rim).astype(BF)
            cross_ref[rows, NF:] = (lim * rre - lre * rim).astype(BF)
    cross = cross_ref[...]
    probe = dot(high_ref[...], cross, NT) + dot(low_ref[...], cross, NT)
    mine = own_block(GROUP * RANK, RANK, GROUP * parts * win, parts * win)
    high, low = split(jnp.where(mine, probe, 0.0))
    raw_ref[...] = (dot(high, cross) + dot(low, cross)).astype(BF)


def cross_and_raw(flat, slots, high, low):
    parts, _, win, _ = flat.shape
    pairs = slots.shape[0] // 2
    rows = GROUP * parts * win
    whole = lambda x: pl.BlockSpec(x.shape, lambda i, s: (0,) * x.ndim)
    return pl.pallas_call(
        cross_kernel,
        grid_spec=pltpu.PrefetchScalarGridSpec(
            num_scalar_prefetch=1,
            grid=(pairs // GROUP,),
            in_specs=[whole(flat), whole(high), whole(low)],
            out_specs=[
                pl.BlockSpec((rows, 2 * NF), lambda i, s: (i, 0)),
                pl.BlockSpec((GROUP * RANK, 2 * NF), lambda i, s: (i, 0)),
            ],
        ),
        out_shape=[
            jax.ShapeDtypeStruct((pairs * parts * win, 2 * NF), BF),
            jax.ShapeDtypeStruct((pairs * RANK, 2 * NF), BF),
        ],
        compiler_params=params(),
        name="cross",
    )(slots, flat, high, low)


def basis_kernel(parts_ref, product_ref, basis_ref, dual_ref):
    raw = parts_ref[0].astype(F32)
    for i in range(1, parts_ref.shape[0]):
        raw = raw + parts_ref[i].astype(F32)
    n = raw.shape[0]
    pairs = n // RANK
    dual = jnp.dot(raw, product_ref[...], precision=HIGHEST, preferred_element_type=F32)
    gram = lax.dot_general(raw, dual, NT, precision=HIGHEST, preferred_element_type=F32)
    gram = jnp.where(own_block(n, RANK, n, RANK), gram, 0.0)
    row = lax.broadcasted_iota(jnp.int32, (n, n), 0)
    col = lax.broadcasted_iota(jnp.int32, (n, n), 1)
    back = jnp.where(row == col, 1.0, 0.0).astype(F32)
    order = lax.broadcasted_iota(jnp.int32, (n, 1), 0) % RANK
    scale = jnp.zeros((n, 1), F32)

    def spread(x, k):
        x = x.reshape(pairs, RANK, x.shape[-1])[:, k : k + 1, :]
        return jnp.broadcast_to(x, (pairs, RANK, x.shape[-1])).reshape(n, x.shape[-1])

    for k in range(RANK):
        column = jnp.sum(jnp.where(col % RANK == k, gram, 0.0), axis=1, keepdims=True)
        pivot = spread(column, k)
        scale = jnp.where(order == k, lax.rsqrt(pivot), scale)
        if k < RANK - 1:
            ratio = jnp.where(order > k, column / pivot, 0.0)
            gram = gram - ratio * spread(gram, k)
            back = back - ratio * spread(back, k)
    back = back * scale
    basis_ref[...] = jnp.dot(back, raw, precision=HIGHEST, preferred_element_type=F32)
    dual_ref[...] = jnp.dot(
        back, dual, precision=HIGHEST, preferred_element_type=F32
    ).astype(BF)


def orthonormal(parts, product):
    n = parts.shape[1]
    return pl.pallas_call(
        basis_kernel,
        out_shape=[
            jax.ShapeDtypeStruct((n, 2 * NF), F32),
            jax.ShapeDtypeStruct((n, 2 * NF), BF),
        ],
        compiler_params=params(),
        name="basis",
    )(parts, product)


def sums_kernel(cross_ref, dual_ref, out_ref):
    cross = cross_ref[...]
    rows = cross.shape[0]
    coeffs = dot(cross, dual_ref[...], NT)
    mine = own_block(rows, rows // GROUP, GROUP * RANK, RANK)
    coeffs = jnp.where(mine, coeffs, 0.0)
    wide = cross.astype(F32)
    energy = jnp.sum(wide * wide, axis=1, keepdims=True)
    out_ref[0, 0:1, :] = jnp.sum(coeffs, axis=0, keepdims=True)
    out_ref[0, 1:2, :] = jnp.sum(coeffs * coeffs, axis=0, keepdims=True)
    out_ref[0, 2:3, :] = jnp.sum(jnp.where(mine, energy, 0.0), axis=0, keepdims=True)


def window_sums(cross, dual):
    steps = dual.shape[0] // (GROUP * RANK)
    rows = cross.shape[0] // steps
    return pl.pallas_call(
        sums_kernel,
        grid=(steps,),
        in_specs=[
            pl.BlockSpec((rows, 2 * NF), lambda i: (i, 0)),
            pl.BlockSpec((GROUP * RANK, 2 * NF), lambda i: (i, 0)),
        ],
        out_specs=pl.BlockSpec((1, 3, GROUP * RANK), lambda i: (i, 0, 0)),
        out_shape=jax.ShapeDtypeStruct((steps, 3, GROUP * RANK), F32),
        compiler_params=params(),
        name="sums",
    )(cross, dual)


def stack_kernel(weights_ref, inverse_ref, out_ref):
    high, low = split(weights_ref[...])
    out_ref[...] = dot(high, inverse_ref[...]) + dot(low, inverse_ref[...])


def stack(weights, inverse):
    pairs = weights.shape[0]
    tile = 512
    return pl.pallas_call(
        stack_kernel,
        grid=(LAGS // tile,),
        in_specs=[
            pl.BlockSpec(weights.shape, lambda i: (0, 0)),
            pl.BlockSpec((2 * NF, tile), lambda i: (0, i)),
        ],
        out_specs=pl.BlockSpec((pairs, tile), lambda i: (0, i)),
        out_shape=jax.ShapeDtypeStruct((pairs, LAGS), F32),
        compiler_params=params(),
        name="stack",
    )(weights, inverse)


def plan(pair_list, n_pair, ch_dev, owner):
    lists = pair_list.reshape(n_pair, 2 * PAIRS_DEV)
    every = jnp.arange(n_pair * ch_dev)
    asked = jnp.any(lists[:, None, :] == every[None, :, None], axis=2)
    blocks = asked.reshape(n_pair, n_pair, ch_dev)
    before = jnp.arange(ch_dev)[None, :] < jnp.arange(ch_dev)[:, None]
    rank = jnp.sum((blocks[:, :, None, :] & before).astype(jnp.int32), axis=3)
    mine = lax.dynamic_slice_in_dim(blocks, owner, 1, 1)[:, 0]
    mine_rank = lax.dynamic_slice_in_dim(rank, owner, 1, 1)[:, 0]
    hit = mine[:, None, :] & (mine_rank[:, None, :] == jnp.arange(CAP)[None, :, None])
    idx = jnp.sum(jnp.where(hit, jnp.arange(ch_dev), 0), axis=2).reshape(-1)
    place = (rank + CAP * jnp.arange(n_pair)[None, :, None]).reshape(n_pair, -1)
    place = lax.dynamic_slice_in_dim(place, owner, 1, 0)[0]
    wanted = lax.dynamic_slice_in_dim(lists, owner, 1, 0)[0]
    slots = jnp.sum(jnp.where(wanted[:, None] == every[None, :], place[None, :], 0), axis=1)
    return idx.astype(jnp.int32), slots.astype(jnp.int32)


def local(forward, inverse, product, records, pair_list, sketch):
    n_pair = lax.axis_size("pair")
    chips = lax.axis_size("chip")
    cores = lax.axis_size("core")
    owner = lax.axis_index("pair")
    core = lax.axis_index("core")
    ch_dev, win, _ = records.shape
    half = PAIRS_DEV // cores
    idx, slots = plan(pair_list, n_pair, ch_dev, owner)
    outgoing = whiten(records, idx, forward)
    arrived = lax.all_to_all(outgoing, "pair", split_axis=0, concat_axis=0, tiled=True)
    arrived = arrived.reshape(n_pair * CAP, win, 2 * NF)
    flat = lax.all_gather(arrived, "core", axis=0)

    probe = jnp.einsum("rl,fl->rf", sketch, inverse.astype(F32), precision=HIGHEST)
    high = lax.reduce_precision(probe, 8, 7)
    low = (probe - high).astype(BF)
    high = jnp.tile(high.astype(BF), (GROUP, 1))
    low = jnp.tile(low, (GROUP, 1))
    slots = lax.dynamic_slice_in_dim(slots, core * half * 2, half * 2, 0)
    cross, raw = cross_and_raw(flat, slots, high, low)
    raw = raw.reshape(chips, half // chips * RANK, 2 * NF)
    parts = lax.all_to_all(raw, "chip", split_axis=0, concat_axis=0, tiled=True)
    basis, dual = orthonormal(parts, product)
    dual = lax.all_gather(dual, "chip", axis=0, tiled=True)
    sums = window_sums(cross, dual)
    sums = jnp.swapaxes(sums, 0, 1).reshape(3, half * RANK)
    sums = lax.psum(sums, "chip")
    own = half // chips * RANK
    sums = lax.dynamic_slice_in_dim(sums, lax.axis_index("chip") * own, own, 1)
    total, power, energy = sums[0], sums[1], sums[2]
    gain = power / (power + energy / (2 * NF))
    windows = win * chips * cores
    weights = (gain * total / windows)[:, None] * basis
    weights = jnp.sum(weights.reshape(half // chips, RANK, 2 * NF), axis=1)
    weights = lax.all_gather(weights, ("chip", "core"), axis=0)
    weights = weights.reshape(chips, cores, half // chips, 2 * NF)
    weights = jnp.swapaxes(weights, 0, 1).reshape(PAIRS_DEV, 2 * NF)
    return stack(weights, inverse)


def solution(mesh):
    n_pair, n_tm = mesh.devices.shape
    fine = Mesh(mesh.devices.reshape(n_pair, n_tm // 2, 2), ("pair", "chip", "core"))
    forward, inverse, product = tables()
    in_specs = (P("pair", ("chip", "core"), None), P(), P())

    def run(records, pair_list, sketch):
        f = functools.partial(
            local, jnp.asarray(forward), jnp.asarray(inverse), jnp.asarray(product)
        )
        return jax.shard_map(
            f, mesh=fine, in_specs=in_specs, out_specs=P("pair", None), check_vma=False
        )(records, pair_list, sketch)

    return run
```

time: 708 us -> 212 us (0.30); the launches traced: 695 us -> 210 us
  other arithmetic: 247 us -> 1.42 us
  waiting for transfers between devices: 229 us -> 44 us
  matrix products: 163 us -> 5.53 us
  blocking collectives: 22.9 us -> 94.3 us
  Pallas kernels: 0 us -> 46.3 us
  local copies, waits for them, and re-layouts: 15.8 us -> 5.06 us
    psum x1 -> x0, waiting for transfers between devices: 219 us -> none  [local(): raw, energy = lax.psum((partial_raw, energy_local), 'tm')]
    another operation x12 -> x0, other arithmetic: 211 us -> none  [the longest x4 188 us: orthonormal(): lower = jnp.linalg.cholesky(gram)]
    dot_general x8 -> x1, matrix products: 141 us -> 5.53 us  [local(): jnp.einsum('rl,fl->rf', sketch, inverse.astype(F32), precision=HIGHEST)]
    all_to_all x0 -> x2, blocking collectives: none -> 68.3 us  [the longest x1 39 us: local(): lax.all_to_all(outgoing, 'pair', split_axis=0, concat_axis=0, tiled=True)]
    pallas_call x0 -> x5, Pallas kernels: none -> 46.3 us  [the longest x1 13 us: orthonormal(): pl.pallas_call(basis_kernel, out_shape=[jax.ShapeDtypeStruct((n, 2 * NF),...]
    all_gather x0 -> x2, waiting for transfers between devices: none -> 43.9 us  [the longest x1 35.8 us: local(): dual = lax.all_gather(dual, 'chip', axis=0, tiled=True)]
    another operation x1 -> x0, matrix products: 21.5 us -> none  [orthonormal(): return lax.linalg.triangular_solve(lower, raw, left_side=True, lower=True)]
    cos x1 -> x0, other arithmetic: 19.4 us -> none  [tables(): jnp.cos(angle)]
  transfers between devices with their start and end apart: 2 -> 2, of which waited for: 2 -> 2; matrix products, arithmetic and copies ran while one was open for 4% -> 3% of each run, Pallas kernels for 0% -> 0%
where the time goes in v1:
time: 212 us; the launch traced here: 210 us
  blocking collectives  94.3 us (44%)
  Pallas kernels  46.3 us (22%)
  waiting for transfers between devices  44 us (21%)
  between operations  13.5 us (6%)
  matrix products  5.53 us (3%)
  local copies, waits for them, and re-layouts  5.06 us (2%)
    all_to_all x1, blocking collectives, local(): lax.all_to_all(outgoing, 'pair', split_axis=0, concat_axis=0, tiled=True)  39 us
    all_gather x1, waiting for transfers between devices, local(): dual = lax.all_gather(dual, 'chip', axis=0, tiled=True)  35.8 us
    all_to_all x1, blocking collectives, local(): parts = lax.all_to_all(raw, 'chip', split_axis=0, concat_axis=0, tiled=True)  29.2 us
    all_gather x1, blocking collectives, local(): weights = lax.all_gather(weights, ('chip', 'core'), axis=0)  14 us
    pallas_call x1, Pallas kernels, orthonormal(): pl.pallas_call(basis_kernel, out_shape=[jax.ShapeDtypeStruct((n, 2 * NF),...  13 us
    psum x1, blocking collectives, local(): sums = lax.psum(sums, 'chip')  12 us
    pallas_call x1, Pallas kernels, cross_and_raw(): pl.pallas_call(cross_kernel, grid_spec=pltpu.PrefetchScalarGridSpec(num_s...  11.8 us
    pallas_call x1, Pallas kernels, whiten(): pl.pallas_call(white_kernel, grid_spec=pltpu.PrefetchScalarGridSpec(num_s...  9.34 us
  transfers between devices with their start and end apart: 2, of which 2 were waited for; matrix products, arithmetic and copies ran while one was open for 3% of the time, Pallas kernels for 0%

profile of v1, /device:TPU:9, one launch (start us, length us, event | category | flops | bytes accessed | tf_op | source)
XLA Modules:
  0.0 210.0 jit_solution(11676190938473235926)
XLA Ops:
  6.6 0.9 copy.14
  7.4 0.2 reshape.75
  7.6 0.2 fusion
  7.8 0.1 and.28
  7.9 0.4 convert_reduce_fusion
  8.3 0.3 select_reduce_fusion.1
  8.6 0.1 copy.15
  8.7 0.6 reshape.76.idx_ref
  9.3 9.3 %whiten.1 = bf16[4,12,16,1024]{3,2,1,0:T(8,128)(2,1)} custom-call(s32[48]{0:T(128)} %reshape.76.idx_ref, bf16[64,16,2048]{2,1,0:T(8,128)(2,1)} %refs_11_.1, bf16[64,16,2048]{2,1,0:T(8,128)(2,1)} %refs_11_.1, bf16[64,16,2048]{2,1,0:T(8,128)(2,1)} %refs_11_.1, bf16[64,16,2048]{2,1,0:T(8,128)(2,1)} %refs_11_.1, bf16[64,16,2048]{2,1,0:T(8,128)(2,1)} %refs_11_.1, ...), custom_call_target="tpu_custom_call" | custom-call | tf_op jit(solution)/shard_map/whiten/pallas_call | solution.py:75
  18.7 39.0 %all_to_all.10 = bf16[4,12,16,1024]{3,2,1,0:T(8,128)(2,1)} all-to-all(bf16[4,12,16,1024]{3,2,1,0:T(8,128)(2,1)} %whiten.1), channel_id=1, replica_groups=mesh['pair'=4,'chip'=4,'core'=2] {'pair'}, dimensions={0} | all-to-all | bytes 3145728 | tf_op jit(solution)/shard_map/all_to_all | solution.py:269
  57.7 0.0 all-gather.4.cloned.1.call-update
  57.7 0.0 all-gather.6.cloned.1.call-start
  57.8 0.1 reduce_sum.39
  57.8 0.1 add.35
  57.9 0.1 add.36
  58.0 0.2 select_reduce_fusion
  58.2 0.7 dynamic_slice.20.slot_ref
  58.9 5.5 %fusion.1 = (bf16[16,1024]{1,0:T(8,128)(2,1)S(1)}, bf16[16,1024]{1,0:T(8,128)(2,1)S(1)}) fusion(bf16[1024,2048]{1,0:T(8,128)(2,1)} %constant.42.clone.inverse_ref, f32[16,2048]{1,0:T(8,128)S(1)} %copy-done), kind=kOutput, calls=%fused_computation.10 | convolution fusion | flops 402718720 | bytes 4390912 | tf_op jit(solution)/shard_map/rl,fl->rf/dot_general | solution.py:273
  64.4 8.2 %all-gather.4.cloned.1.call-done.flat_ref = bf16[2,48,16,1024]{3,2,1,0:T(8,128)(2,1)} async-done(((bf16[1,48,16,1024]{3,2,1,0:T(8,128)(2,1)}), bf16[2,48,16,1024]{3,2,1,0:T(8,128)(2,1)}) %all-gather.4.cloned.1.call-update) | async-done | bytes 3145744 | tf_op jit(solution)/shard_map/all_gather | solution.py:271
  72.6 0.7 tile.8
  73.3 0.7 tile.20
  74.0 11.8 %cross.1 = (bf16[2048,1024]{1,0:T(8,128)(2,1)}, bf16[1024,1024]{1,0:T(8,128)(2,1)}) custom-call(s32[128]{0:T(128)} %dynamic_slice.20.slot_ref, bf16[2,48,16,1024]{3,2,1,0:T(8,128)(2,1)} %all-gather.4.cloned.1.call-done.flat_ref, bf16[128,1024]{1,0:T(8,128)(2,1)} %bitcast.30, bf16[128,1024]{1,0:T(8,128)(2,1)} %bitcast.31), custom_call_target="tpu_custom_call" | custom-call | tf_op jit(solution)/shard_map/cross/pallas_call | solution.py:122
  85.8 29.2 %all_to_all.11.parts_ref = bf16[4,256,1024]{2,1,0:T(8,128)(2,1)} all-to-all(bf16[4,256,1024]{2,1,0:T(8,128)(2,1)} %bitcast.27), channel_id=1, replica_groups=mesh['pair'=4,'chip'=4,'core'=2] {'chip'}, dimensions={0} | all-to-all | bytes 4194304 | tf_op jit(solution)/shard_map/all_to_all | solution.py:281
  115.1 13.0 %basis.1 = (f32[256,1024]{1,0:T(8,128)}, bf16[256,1024]{1,0:T(8,128)(2,1)}) custom-call(bf16[4,256,1024]{2,1,0:T(8,128)(2,1)} %all_to_all.11.parts_ref, f32[1024,1024]{1,0:T(8,128)} %constant.43.clone.product_ref), custom_call_target="tpu_custom_call" | custom-call | tf_op jit(solution)/shard_map/basis/pallas_call | solution.py:178
  128.1 35.8 %all-gather.6.cloned.1.call-done.dual_ref = bf16[1024,1024]{1,0:T(8,128)(2,1)} async-done(((bf16[256,1024]{1,0:T(8,128)(2,1)}), bf16[1024,1024]{1,0:T(8,128)(2,1)}) %all-gather.6.cloned.1.call-update) | async-done | bytes 2097168 | tf_op jit(solution)/shard_map/all_gather | solution.py:283
  163.9 7.1 %sums.1 = f32[8,3,128]{2,1,0:T(4,128)} custom-call(bf16[2048,1024]{1,0:T(8,128)(2,1)} %get-tuple-element.9.cross_ref, bf16[1024,1024]{1,0:T(8,128)(2,1)} %all-gather.6.cloned.1.call-done.dual_ref), custom_call_target="tpu_custom_call" | custom-call | tf_op jit(solution)/shard_map/sums/pallas_call | solution.py:205
  171.0 12.0 %psum.7 = f32[3,1024]{1,0:T(4,128)S(1)} all-reduce(f32[3,1024]{1,0:T(4,128)} %bitcast.32), channel_id=1, replica_groups=mesh['pair'=4,'chip'=4,'core'=2] {'chip'}, use_global_device_ids=true, to_apply=%region_4.5 | all-reduce | flops 3072 | bytes 24576 | tf_op jit(solution)/shard_map/psum | solution.py:286
  183.0 0.1 dynamic-slice_multiply_fusion
  183.1 0.3 bitcast_reduce_fusion
  183.4 14.0 %all-gather = f32[128,1024]{1,0:T(8,128)S(1)} all-gather(f32[16,1024]{1,0:T(8,128)S(1)} %bitcast_reduce_fusion), channel_id=2, replica_groups=mesh['pair'=4,'chip'=4,'core'=2] {'chip','core'}, dimensions={0}, use_global_device_ids=true | all-gather | bytes 589824 | tf_op jit(solution)/shard_map/all_gather | solution.py:294
  197.4 0.8 copy.16
  198.2 5.0 %stack.1 = f32[128,2048]{1,0:T(8,128)} custom-call(f32[128,1024]{1,0:T(8,128)} %bitcast.29, bf16[1024,2048]{1,0:T(8,128)(2,1)} %constant.42.clone.inverse_ref), custom_call_target="tpu_custom_call" | custom-call | tf_op jit(solution)/shard_map/stack/pallas_call | solution.py:227
  (13 shorter events, 0.1 us)
Async XLA Ops:
  6.5 52.3 %copy-start = (f32[16,2048]{1,0:T(8,128)S(1)}, f32[16,2048]{1,0:T(8,128)}, u32[]{:S(2)}) copy-start(f32[16,2048]{1,0:T(8,128)} %param.8) | copy-start | bytes 393220
  6.5 66.0 %all-gather.4.cloned.1.call-start = ((), (), s32[]{:S(2)}) async-start(), calls=%async_computation.2 | async-start | bytes 4718592 | tf_op jit(solution)/shard_map/all_gather | solution.py:271
  57.7 106.2 %all-gather.6.cloned.1.call-start = ((), (), s32[]{:S(2)}) async-start(), calls=%async_computation.3 | async-start | bytes 2621440 | tf_op jit(solution)/shard_map/all_gather | solution.py:283
  128.1 55.0 %copy-start.1 = (f32[256,1024]{1,0:T(8,128)S(1)}, f32[256,1024]{1,0:T(8,128)}, u32[]{:S(2)}) copy-start(f32[256,1024]{1,0:T(8,128)} %get-tuple-element.12) | copy-start | bytes 3145732
Sparse Core Ops, SparseCore 0:
  57.8 14.7 all-gather.3
  128.3 35.6 all-gather.5

commit v2 on v1

v2 whole, which is shorter than its diff:
```python
import functools
import math

import jax
import jax.numpy as jnp
import numpy as np
from jax import lax
from jax.experimental import pallas as pl
from jax.experimental.pallas import tpu as pltpu
from jax.sharding import Mesh
from jax.sharding import PartitionSpec as P

SAMPLES = 2048
NF = 512
LAGS = 2048
RANK = 16
CAP = 12
PAIRS_DEV = 128
GROUP = 8
BF = jnp.bfloat16
F32 = jnp.float32
HIGHEST = lax.Precision.HIGHEST
VMEM = 56 * 1024 * 1024
NT = (((1,), (1,)), ((), ()))


def tables():
    freq = NF // 2 + np.arange(NF)
    scale = np.float32(2.0 * math.pi / SAMPLES)
    times = np.arange(SAMPLES)
    turn = np.mod(times[:, None] * freq[None, :], SAMPLES).astype(np.float32) * scale
    forward = np.concatenate([np.cos(turn), np.sin(turn)], axis=1).astype(jnp.bfloat16)
    shifts = np.arange(LAGS) - LAGS // 2
    angle = np.mod(freq[:, None] * shifts[None, :], SAMPLES).astype(np.float32) * scale
    inverse = (
        np.concatenate([np.cos(angle), -np.sin(angle)], axis=0) / np.float32(math.sqrt(NF))
    ).astype(jnp.bfloat16)
    wide = inverse.astype(np.float64)
    return forward, inverse, (wide @ wide.T).astype(np.float32)


def split(x):
    high = x.astype(BF)
    return high, (x - high.astype(F32)).astype(BF)


def dot(a, b, dims=(((1,), (0,)), ((), ()))):
    return lax.dot_general(a, b, dims, preferred_element_type=F32)


def params():
    return pltpu.CompilerParams(vmem_limit_bytes=VMEM)


MESH = pl.DeviceIdType.MESH


def own_block(rows, row_size, cols, col_size):
    r = lax.broadcasted_iota(jnp.int32, (rows, cols), 0) // row_size
    c = lax.broadcasted_iota(jnp.int32, (rows, cols), 1) // col_size
    return r == c


def partner(me, k, n):
    out = 0
    bit = 1
    while bit < n:
        digit = (me // bit) % 2
        out = out + bit * (1 - digit if (k // bit) % 2 else digit)
        bit *= 2
    return out


def greet(others):
    barrier = pltpu.get_barrier_semaphore()
    for device in others:
        pl.semaphore_signal(barrier, inc=1, device_id=device, device_id_type=MESH)
    pl.semaphore_wait(barrier, len(others))


def send(src, dst, sems, at, device):
    copy = pltpu.make_async_remote_copy(
        src_ref=src,
        dst_ref=dst,
        send_sem=sems[0].at[at],
        recv_sem=sems[1].at[at],
        device_id=device,
        device_id_type=MESH,
    )
    copy.start()
    return copy


def white_kernel(n, idx_ref, records_ref, forward_ref, flat_ref, out_buf, zs, zr, cs, cr):
    me = lax.axis_index("pair")
    core = lax.axis_index("core")
    sibling = {"core": 1 - core}
    greet([{"pair": partner(me, k, n)} for k in range(1, n)] + [sibling])

    def whitened(d, put):
        block = jnp.concatenate([records_ref[idx_ref[d * CAP + j]] for j in range(CAP)], axis=0)
        spectra = dot(block, forward_ref[...])
        re, im = spectra[:, :NF], spectra[:, NF:]
        power = re * re + im * im
        level = jnp.mean(power, axis=1, keepdims=True)
        factor = lax.rsqrt(power + level + 1e-06)
        win = block.shape[0] // CAP
        put(0, (re * factor).astype(BF).reshape(CAP, win, NF))
        put(NF, (im * factor).astype(BF).reshape(CAP, win, NF))

    order = list(range(n // 2, n)) + list(range(1, n // 2))
    copies = {}
    for k in order:
        d = partner(me, k, n)

        def put(at, value, k=k):
            out_buf[k - 1, :, :, at : at + NF] = value

        whitened(d, put)
        copies[k] = send(out_buf.at[k - 1], flat_ref.at[core, me], (zs, zr), k - 1, {"pair": d})

    def put_own(at, value):
        flat_ref[core, me, :, :, at : at + NF] = value

    whitened(me, put_own)
    shared = [send(flat_ref.at[core, me], flat_ref.at[core, me], (cs, cr), 0, sibling)]
    for k in [*range(1, n // 2), *range(n // 2, n)]:
        copies[k].wait_recv()
        block = flat_ref.at[core, partner(me, k, n)]
        shared.append(send(block, block, (cs, cr), k, sibling))
    for k in order:
        copies[k].wait_send()
    for copy in shared:
        copy.wait()


def white_exchange(records, idx, forward):
    _, win, _ = records.shape
    n = idx.shape[0] // CAP
    vmem = pl.BlockSpec(memory_space=pltpu.VMEM)
    return pl.pallas_call(
        functools.partial(white_kernel, n),
        in_specs=[pl.BlockSpec(memory_space=pltpu.SMEM), vmem, vmem],
        out_specs=vmem,
        out_shape=jax.ShapeDtypeStruct((2, n, CAP, win, 2 * NF), BF),
        scratch_shapes=[
            pltpu.VMEM((n - 1, CAP, win, 2 * NF), BF),
            pltpu.SemaphoreType.DMA((n - 1,)),
            pltpu.SemaphoreType.DMA((n - 1,)),
            pltpu.SemaphoreType.DMA((n,)),
            pltpu.SemaphoreType.DMA((n,)),
        ],
        compiler_params=pltpu.CompilerParams(
            vmem_limit_bytes=VMEM, collective_id=0, has_side_effects=True
        ),
        name="white_exchange",
    )(idx, records, forward)


def full(a, b, dims=(((1,), (0,)), ((), ()))):
    return lax.dot_general(a, b, dims, precision=HIGHEST, preferred_element_type=F32)


def eliminate(gram):
    n = gram.shape[0]
    pairs = n // RANK
    row = lax.broadcasted_iota(jnp.int32, (n, n), 0)
    col = lax.broadcasted_iota(jnp.int32, (n, n), 1)
    gram = jnp.where(row // RANK == col // RANK, gram, 0.0)
    back = jnp.where(row == col, 1.0, 0.0).astype(F32)
    order = lax.broadcasted_iota(jnp.int32, (n, 1), 0) % RANK
    scale = jnp.zeros((n, 1), F32)

    def spread(x, k):
        x = x.reshape(pairs, RANK, x.shape[-1])[:, k : k + 1, :]
        return jnp.broadcast_to(x, (pairs, RANK, x.shape[-1])).reshape(n, x.shape[-1])

    for k in range(RANK):
        column = jnp.sum(jnp.where(col % RANK == k, gram, 0.0), axis=1, keepdims=True)
        pivot = spread(column, k)
        scale = jnp.where(order == k, lax.rsqrt(pivot), scale)
        if k < RANK - 1:
            ratio = jnp.where(order > k, column / pivot, 0.0)
            gram = gram - ratio * spread(gram, k)
            back = back - ratio * spread(back, k)
    return back * scale


def pair_kernel(
    chips, windows, slot_ref, flat_ref, high_ref, low_ref, product_ref, out_ref,
    cross_ref, raw_buf, raw_in, energy_ref, dual_ref, sums_buf, sums_in,
    rs, rr, ds, dr, ss, sr, ws, wr,
):
    me = lax.axis_index("chip")
    core = lax.axis_index("core")
    there = [partner(me, k, chips) for k in range(chips)]
    groups = sums_buf.shape[1]
    lanes = GROUP * RANK
    _, _, win, _ = flat_ref.shape
    rows = GROUP * 2 * win
    everyone = [(k, c) for k in range(chips) for c in range(2) if k or c]

    def device(k, c):
        return {"chip": there[k], "core": 1 - core if c else core}

    greet([device(k, c) for k, c in everyone])
    order = list(range(chips - 1, 0, -1))

    sent = {}
    for k in order + [0]:
        for g in range(groups):
            step = there[k] * groups + g

            @pl.loop(0, GROUP)
            def _(q, step=step):
                a = slot_ref[(step * GROUP + q) * 2]
                b = slot_ref[(step * GROUP + q) * 2 + 1]
                for part in range(2):
                    left = flat_ref[part, a].astype(F32)
                    right = flat_ref[part, b].astype(F32)
                    lre, lim = left[:, :NF], left[:, NF:]
                    rre, rim = right[:, :NF], right[:, NF:]
                    at = pl.ds(pl.multiple_of((q * 2 + part) * win, 16), win)
                    cross_ref[step, at, :NF] = (lre * rre + lim * rim).astype(BF)
                    cross_ref[step, at, NF:] = (lim * rre - lre * rim).astype(BF)

            cross = cross_ref[step]
            probe = dot(high_ref[...], cross, NT) + dot(low_ref[...], cross, NT)
            high, low = split(jnp.where(own_block(lanes, RANK, rows, 2 * win), probe, 0.0))
            raw = dot(high, cross) + dot(low, cross)
            raw_buf[k, g * lanes : (g + 1) * lanes, :] = raw.astype(BF)
            wide = cross.astype(F32)
            energy = jnp.sum(wide * wide, axis=1, keepdims=True)
            energy = jnp.where(own_block(rows, 2 * win, lanes, RANK), energy, 0.0)
            energy_ref[step] = jnp.sum(energy, axis=0, keepdims=True)
        if k:
            sent[k] = send(raw_buf.at[k], raw_in.at[k - 1], (rs, rr), k - 1, device(k, 0))

    raw = raw_buf[0].astype(F32)
    for k in order:
        sent[k].wait()
        raw = raw + raw_in[k - 1].astype(F32)
    dual = full(raw, product_ref[...])
    back = eliminate(full(raw, dual, NT))
    dual_ref[0] = full(back, dual).astype(BF)
    sent = {}
    for k in order:
        sent[k] = send(dual_ref.at[0], dual_ref.at[k], (ds, dr), k - 1, device(k, 0))

    summed = {}
    for k in [0] + order[::-1]:
        if k:
            sent[k].wait()
        for g in range(groups):
            step = there[k] * groups + g
            part = dual_ref[k, g * lanes : (g + 1) * lanes, :]
            coeffs = dot(cross_ref[step], part, NT)
            coeffs = jnp.where(own_block(rows, 2 * win, lanes, RANK), coeffs, 0.0)
            total = jnp.sum(coeffs, axis=0, keepdims=True)
            power = jnp.sum(coeffs * coeffs, axis=0, keepdims=True)
            pad = jnp.zeros((5, lanes), F32)
            sums_buf[k, g] = jnp.concatenate([total, power, energy_ref[step], pad], axis=0)
        if k:
            summed[k] = send(sums_buf.at[k], sums_in.at[k - 1], (ss, sr), k - 1, device(k, 0))
    sums = sums_buf[0]
    for k in order[::-1]:
        summed[k].wait()
        sums = sums + sums_in[k - 1]
    total, power, energy = sums[:, 0:1, :], sums[:, 1:2, :], sums[:, 2:3, :]
    weight = power / (power + energy / (2 * NF)) * total / windows
    weight = jnp.concatenate([weight[g] for g in range(groups)], axis=1)
    pairs = groups * GROUP
    weight = jnp.where(own_block(pairs, 1, pairs * RANK, RANK), weight, 0.0)
    out_ref[core, me] = full(full(weight, back), raw)
    mine = out_ref.at[core, me]
    last = [send(mine, mine, (ws, wr), 2 * k + c - 1, device(k, c)) for k, c in everyone]
    for copy in last:
        copy.wait()


def pair_weights(flat, slots, high, low, product, chips, windows):
    parts, _, win, _ = flat.shape
    pairs = slots.shape[0] // 2
    groups = pairs // chips // GROUP
    lanes = GROUP * RANK
    steps = pairs // GROUP
    vmem = pl.BlockSpec(memory_space=pltpu.VMEM)
    dma = pltpu.SemaphoreType.DMA
    return pl.pallas_call(
        functools.partial(pair_kernel, chips, windows),
        in_specs=[pl.BlockSpec(memory_space=pltpu.SMEM)] + [vmem] * 4,
        out_specs=vmem,
        out_shape=jax.ShapeDtypeStruct((2, chips, pairs // chips, 2 * NF), F32),
        scratch_shapes=[
            pltpu.VMEM((steps, GROUP * parts * win, 2 * NF), BF),
            pltpu.VMEM((chips, groups * lanes, 2 * NF), BF),
            pltpu.VMEM((chips - 1, groups * lanes, 2 * NF), BF),
            pltpu.VMEM((steps, 1, lanes), F32),
            pltpu.VMEM((chips, groups * lanes, 2 * NF), BF),
            pltpu.VMEM((chips, groups, 8, lanes), F32),
            pltpu.VMEM((chips - 1, groups, 8, lanes), F32),
        ]
        + [dma((chips - 1,))] * 6
        + [dma((2 * chips - 1,))] * 2,
        compiler_params=pltpu.CompilerParams(
            vmem_limit_bytes=VMEM, collective_id=1, has_side_effects=True
        ),
        name="pair_weights",
    )(slots, flat, high, low, product)


def stack_kernel(weights_ref, inverse_ref, out_ref):
    high, low = split(weights_ref[...])
    out_ref[...] = dot(high, inverse_ref[...]) + dot(low, inverse_ref[...])


def stack(weights, inverse):
    pairs = weights.shape[0]
    tile = 512
    return pl.pallas_call(
        stack_kernel,
        grid=(LAGS // tile,),
        in_specs=[
            pl.BlockSpec(weights.shape, lambda i: (0, 0)),
            pl.BlockSpec((2 * NF, tile), lambda i: (0, i)),
        ],
        out_specs=pl.BlockSpec((pairs, tile), lambda i: (0, i)),
        out_shape=jax.ShapeDtypeStruct((pairs, LAGS), F32),
        compiler_params=params(),
        name="stack",
    )(weights, inverse)


def plan(pair_list, n_pair, ch_dev, owner):
    lists = pair_list.reshape(n_pair, 2 * PAIRS_DEV)
    every = jnp.arange(n_pair * ch_dev)
    asked = jnp.any(lists[:, None, :] == every[None, :, None], axis=2)
    blocks = asked.reshape(n_pair, n_pair, ch_dev)
    before = jnp.arange(ch_dev)[None, :] < jnp.arange(ch_dev)[:, None]
    rank = jnp.sum((blocks[:, :, None, :] & before).astype(jnp.int32), axis=3)
    mine = lax.dynamic_slice_in_dim(blocks, owner, 1, 1)[:, 0]
    mine_rank = lax.dynamic_slice_in_dim(rank, owner, 1, 1)[:, 0]
    hit = mine[:, None, :] & (mine_rank[:, None, :] == jnp.arange(CAP)[None, :, None])
    idx = jnp.sum(jnp.where(hit, jnp.arange(ch_dev), 0), axis=2).reshape(-1)
    place = (rank + CAP * jnp.arange(n_pair)[None, :, None]).reshape(n_pair, -1)
    place = lax.dynamic_slice_in_dim(place, owner, 1, 0)[0]
    wanted = lax.dynamic_slice_in_dim(lists, owner, 1, 0)[0]
    slots = jnp.sum(jnp.where(wanted[:, None] == every[None, :], place[None, :], 0), axis=1)
    return idx.astype(jnp.int32), slots.astype(jnp.int32)


def local(forward, inverse, product, records, pair_list, sketch):
    n_pair = lax.axis_size("pair")
    chips = lax.axis_size("chip")
    cores = lax.axis_size("core")
    owner = lax.axis_index("pair")
    core = lax.axis_index("core")
    ch_dev, win, _ = records.shape
    half = PAIRS_DEV // cores
    idx, slots = plan(pair_list, n_pair, ch_dev, owner)
    flat = white_exchange(records, idx, forward)
    flat = flat.reshape(cores, n_pair * CAP, win, 2 * NF)

    probe = jnp.einsum("rl,fl->rf", sketch, inverse.astype(F32), precision=HIGHEST)
    high = lax.reduce_precision(probe, 8, 7)
    low = (probe - high).astype(BF)
    high = jnp.tile(high.astype(BF), (GROUP, 1))
    low = jnp.tile(low, (GROUP, 1))
    slots = lax.dynamic_slice_in_dim(slots, core * half * 2, half * 2, 0)
    weights = pair_weights(flat, slots, high, low, product, chips, win * chips * cores)
    return stack(weights.reshape(PAIRS_DEV, 2 * NF), inverse)


def solution(mesh):
    n_pair, n_tm = mesh.devices.shape
    fine = Mesh(mesh.devices.reshape(n_pair, n_tm // 2, 2), ("pair", "chip", "core"))
    forward, inverse, product = tables()
    in_specs = (P("pair", ("chip", "core"), None), P(), P())

    def run(records, pair_list, sketch):
        f = functools.partial(
            local, jnp.asarray(forward), jnp.asarray(inverse), jnp.asarray(product)
        )
        return jax.shard_map(
            f, mesh=fine, in_specs=in_specs, out_specs=P("pair", None), check_vma=False
        )(records, pair_list, sketch)

    return run
```

time: 212 us -> 140 us (0.66)
  blocking collectives: 94.3 us -> 0 us
  Pallas kernels: 46.3 us -> 129 us
  waiting for transfers between devices: 44 us -> 0 us
  between operations: 13.5 us -> 0.07 us
    pallas_call x4 -> x2, Pallas kernels: 41.3 us -> 124 us  [the longest x1 78.3 us: pair_weights(): pl.pallas_call(functools.partial(pair_kernel, chips, windows), in_specs=[...]
    all_to_all x2 -> x0, blocking collectives: 68.3 us -> none  [the longest x1 39 us: local(): lax.all_to_all(outgoing, 'pair', split_axis=0, concat_axis=0, tiled=True)]
    all_gather x2 -> x0, waiting for transfers between devices: 43.9 us -> none  [the longest x1 35.8 us: local(): dual = lax.all_gather(dual, 'chip', axis=0, tiled=True)]
    all_gather x1 -> x0, blocking collectives: 14 us -> none  [local(): weights = lax.all_gather(weights, ('chip', 'core'), axis=0)]
    psum x1 -> x0, blocking collectives: 12 us -> none  [local(): sums = lax.psum(sums, 'chip')]
  transfers between devices with their start and end apart: 2 -> 0, of which waited for: 2 -> 0; matrix products, arithmetic and copies ran while one was open for 3% -> 0% of each run, Pallas kernels for 0% -> 0%
where the time goes in v2:
time: 140 us
  Pallas kernels  129 us (92%)
  matrix products  5.53 us (4%)
  local copies, waits for them, and re-layouts  4.14 us (3%)
    pallas_call x1, Pallas kernels, pair_weights(): pl.pallas_call(functools.partial(pair_kernel, chips, windows), in_specs=[...  78.3 us
    pallas_call x1, Pallas kernels, white_exchange(): pl.pallas_call(functools.partial(white_kernel, n), in_specs=[pl.BlockSpec...  45.6 us
    dot_general x1, matrix products, local(): jnp.einsum('rl,fl->rf', sketch, inverse.astype(F32), precision=HIGHEST)  5.53 us
    pallas_call x1, Pallas kernels, stack(): pl.pallas_call(stack_kernel, grid=(LAGS // tile,), in_specs=[pl.BlockSpec...  4.99 us

profile of v2, /device:TPU:9, one launch (start us, length us, event | category | flops | bytes accessed | tf_op | source)
XLA Modules:
  0.0 139.7 jit_solution(15701831138924351901)
XLA Ops:
  0.0 0.0 copy-start
  0.0 0.0 copy-start.1
  0.0 0.1 add.23
  0.1 0.1 add.24
  0.2 0.7 copy-done
  0.9 5.5 %fusion.1 = (bf16[16,1024]{1,0:T(8,128)(2,1)S(1)}, bf16[16,1024]{1,0:T(8,128)(2,1)S(1)}) fusion(bf16[1024,2048]{1,0:T(8,128)(2,1)} %constant.30.clone.inverse_ref, f32[16,2048]{1,0:T(8,128)S(1)} %copy-done), kind=kOutput, calls=%fused_computation.8 | convolution fusion | flops 402718720 | bytes 4390912 | tf_op jit(solution)/shard_map/rl,fl->rf/dot_general | solution.py:364
  6.4 0.7 tile.20
  7.2 0.7 tile.8
  7.9 0.0 copy-done.1
  7.9 0.1 copy.10
  8.1 0.2 reshape.44
  8.2 0.2 fusion
  8.5 0.1 and.27
  8.5 0.4 convert_reduce_fusion
  9.0 0.1 reduce_sum.30
  9.1 0.2 select_reduce_fusion
  9.2 0.6 dynamic_slice.17.slot_ref
  9.9 0.3 select_reduce_fusion.1
  10.1 0.1 copy.11
  10.2 0.6 reshape.45.idx_ref
  10.8 45.6 %white_exchange.1 = bf16[2,4,12,16,1024]{4,3,2,1,0:T(8,128)(2,1)} custom-call(s32[48]{0:T(128)} %reshape.45.idx_ref, bf16[64,16,2048]{2,1,0:T(8,128)(2,1)} %records_ref.1, bf16[2048,1024]{1,0:T(8,128)(2,1)} %constant.29.clone.forward_ref), custom_call_target="tpu_custom_call" | custom-call | tf_op jit(solution)/shard_map/white_exchange/pallas_call | solution.py:141
  56.4 78.3 %pair_weights.1 = f32[2,4,16,1024]{3,2,1,0:T(8,128)} custom-call(s32[128]{0:T(128)} %dynamic_slice.17.slot_ref, bf16[2,48,16,1024]{3,2,1,0:T(8,128)(2,1)} %bitcast.14, bf16[128,1024]{1,0:T(8,128)(2,1)} %bitcast.17, bf16[128,1024]{1,0:T(8,128)(2,1)} %bitcast.16, f32[1024,1024]{1,0:T(8,128)} %constant.31.clone.product_ref), custom_call_target="tpu_custom_call" | custom-call | tf_op jit(solution)/shard_map/pair_weights/pallas_call | solution.py:289
  134.7 5.0 %stack.1 = f32[128,2048]{1,0:T(8,128)} custom-call(f32[128,1024]{1,0:T(8,128)} %bitcast.15, bf16[1024,2048]{1,0:T(8,128)(2,1)} %constant.30.clone.inverse_ref), custom_call_target="tpu_custom_call" | custom-call | tf_op jit(solution)/shard_map/stack/pallas_call | solution.py:320
  (6 shorter events, 0.1 us)
Async XLA Ops:
  0.0 0.9 copy-start
  0.0 7.9 %copy-start.1 = (s32[512,2]{0,1:T(2,128)S(1)}, s32[512,2]{0,1:T(2,128)}, u32[]{:S(2)}) copy-start(s32[512,2]{0,1:T(2,128)} %param.7) | copy-start | bytes 12292

commit v3 on v2

--- a/solution.py
+++ b/solution.py
@@ -36,7 +36,10 @@
         np.concatenate([np.cos(angle), -np.sin(angle)], axis=0) / np.float32(math.sqrt(NF))
     ).astype(jnp.bfloat16)
     wide = inverse.astype(np.float64)
-    return forward, inverse, (wide @ wide.T).astype(np.float32)
+    product = (wide @ wide.T).astype(np.float32)
+    high = product.astype(jnp.bfloat16)
+    low = (product - high.astype(np.float32)).astype(jnp.bfloat16)
+    return forward, inverse, np.stack([high, low])
 
 
 def split(x):
@@ -91,72 +94,6 @@
     return copy
 
 
-def white_kernel(n, idx_ref, records_ref, forward_ref, flat_ref, out_buf, zs, zr, cs, cr):
-    me = lax.axis_index("pair")
-    core = lax.axis_index("core")
-    sibling = {"core": 1 - core}
-    greet([{"pair": partner(me, k, n)} for k in range(1, n)] + [sibling])
-
-    def whitened(d, put):
-        block = jnp.concatenate([records_ref[idx_ref[d * CAP + j]] for j in range(CAP)], axis=0)
-        spectra = dot(block, forward_ref[...])
-        re, im = spectra[:, :NF], spectra[:, NF:]
-        power = re * re + im * im
-        level = jnp.mean(power, axis=1, keepdims=True)
-        factor = lax.rsqrt(power + level + 1e-06)
-        win = block.shape[0] // CAP
-        put(0, (re * factor).astype(BF).reshape(CAP, win, NF))
-        put(NF, (im * factor).astype(BF).reshape(CAP, win, NF))
-
-    order = list(range(n // 2, n)) + list(range(1, n // 2))
-    copies = {}
-    for k in order:
-        d = partner(me, k, n)
-
-        def put(at, value, k=k):
-            out_buf[k - 1, :, :, at : at + NF] = value
-
-        whitened(d, put)
-        copies[k] = send(out_buf.at[k - 1], flat_ref.at[core, me], (zs, zr), k - 1, {"pair": d})
-
-    def put_own(at, value):
-        flat_ref[core, me, :, :, at : at + NF] = value
-
-    whitened(me, put_own)
-    shared = [send(flat_ref.at[core, me], flat_ref.at[core, me], (cs, cr), 0, sibling)]
-    for k in [*range(1, n // 2), *range(n // 2, n)]:
-        copies[k].wait_recv()
-        block = flat_ref.at[core, partner(me, k, n)]
-        shared.append(send(block, block, (cs, cr), k, sibling))
-    for k in order:
-        copies[k].wait_send()
-    for copy in shared:
-        copy.wait()
-
-
-def white_exchange(records, idx, forward):
-    _, win, _ = records.shape
-    n = idx.shape[0] // CAP
-    vmem = pl.BlockSpec(memory_space=pltpu.VMEM)
-    return pl.pallas_call(
-        functools.partial(white_kernel, n),
-        in_specs=[pl.BlockSpec(memory_space=pltpu.SMEM), vmem, vmem],
-        out_specs=vmem,
-        out_shape=jax.ShapeDtypeStruct((2, n, CAP, win, 2 * NF), BF),
-        scratch_shapes=[
-            pltpu.VMEM((n - 1, CAP, win, 2 * NF), BF),
-            pltpu.SemaphoreType.DMA((n - 1,)),
-            pltpu.SemaphoreType.DMA((n - 1,)),
-            pltpu.SemaphoreType.DMA((n,)),
-            pltpu.SemaphoreType.DMA((n,)),
-        ],
-        compiler_params=pltpu.CompilerParams(
-            vmem_limit_bytes=VMEM, collective_id=0, has_side_effects=True
-        ),
-        name="white_exchange",
-    )(idx, records, forward)
-
-
 def full(a, b, dims=(((1,), (0,)), ((), ()))):
     return lax.dot_general(a, b, dims, precision=HIGHEST, preferred_element_type=F32)
 
@@ -186,29 +123,89 @@
     return back * scale
 
 
-def pair_kernel(
-    chips, windows, slot_ref, flat_ref, high_ref, low_ref, product_ref, out_ref,
-    cross_ref, raw_buf, raw_in, energy_ref, dual_ref, sums_buf, sums_in,
-    rs, rr, ds, dr, ss, sr, ws, wr,
+def kernel(
+    n, chips, windows, idx_ref, slot_ref, records_ref, forward_ref, sketch_ref, inverse_hbm,
+    product_hbm, out_ref, inverse_ref, product_ref, white_buf, flat_ref, probe_ref, cross_ref,
+    raw_buf, raw_in, energy_ref, dual_ref, sums_buf, sums_in,
+    load, zs, zr, cs, cr, rs, rr, ds, dr, ss, sr, ws, wr,
 ):
+    owner = lax.axis_index("pair")
     me = lax.axis_index("chip")
     core = lax.axis_index("core")
     there = [partner(me, k, chips) for k in range(chips)]
     groups = sums_buf.shape[1]
     lanes = GROUP * RANK
-    _, _, win, _ = flat_ref.shape
+    win = records_ref.shape[1]
     rows = GROUP * 2 * win
     everyone = [(k, c) for k in range(chips) for c in range(2) if k or c]
 
     def device(k, c):
         return {"chip": there[k], "core": 1 - core if c else core}
 
-    greet([device(k, c) for k, c in everyone])
+    loads = [
+        pltpu.make_async_copy(inverse_hbm, inverse_ref, load.at[0]),
+        pltpu.make_async_copy(product_hbm, product_ref, load.at[1]),
+    ]
+    for copy in loads:
+        copy.start()
+    greet(
+        [{"pair": partner(owner, k, n)} for k in range(1, n)] + [device(k, c) for k, c in everyone]
+    )
+
+    def slots_of(o):
+        return pl.ds(pl.multiple_of(o * CAP, CAP), CAP)
+
+    def whitened(d, put):
+        block = jnp.concatenate([records_ref[idx_ref[d * CAP + j]] for j in range(CAP)], axis=0)
+        spectra = dot(block, forward_ref[...])
+        re, im = spectra[:, :NF], spectra[:, NF:]
+        power = re * re + im * im
+        level = jnp.mean(power, axis=1, keepdims=True)
+        factor = lax.rsqrt(power + level + 1e-06)
+        put(0, (re * factor).astype(BF).reshape(CAP, win, NF))
+        put(NF, (im * factor).astype(BF).reshape(CAP, win, NF))
+
+    far_first = list(range(n // 2, n)) + list(range(1, n // 2))
+    copies = {}
+    for k in far_first:
+        d = partner(owner, k, n)
+
+        def put(at, value, k=k):
+            white_buf[k - 1, :, :, at : at + NF] = value
+
+        whitened(d, put)
+        copies[k] = send(
+            white_buf.at[k - 1], flat_ref.at[core, slots_of(owner)], (zs, zr), k - 1, {"pair": d}
+        )
+
+    def put_own(at, value):
+        flat_ref[core, slots_of(owner), :, at : at + NF] = value
+
+    whitened(owner, put_own)
+    block = flat_ref.at[core, slots_of(owner)]
+    shared = [send(block, block, (cs, cr), 0, device(0, 1))]
+
+    loads[0].wait()
+    first = sketch_ref[...].astype(BF)
+    second, third = split(sketch_ref[...] - first.astype(F32))
+    probes = dot(jnp.concatenate([first, second, third], axis=0), inverse_ref[...], NT)
+    high, low = split(probes[:RANK] + probes[RANK : 2 * RANK] + probes[2 * RANK :])
+    probe_ref[0] = jnp.concatenate([high] * GROUP, axis=0)
+    probe_ref[1] = jnp.concatenate([low] * GROUP, axis=0)
+
+    for k in [*range(1, n // 2), *range(n // 2, n)]:
+        copies[k].wait_recv()
+        block = flat_ref.at[core, slots_of(partner(owner, k, n))]
+        shared.append(send(block, block, (cs, cr), k, device(0, 1)))
+    for k in far_first:
+        copies[k].wait_send()
+    for copy in shared:
+        copy.wait()
+
     order = list(range(chips - 1, 0, -1))
-
     sent = {}
-    for k in order + [0]:
-        for g in range(groups):
+    for g in range(groups):
+        for k in order + [0]:
             step = there[k] * groups + g
 
             @pl.loop(0, GROUP)
@@ -225,41 +222,63 @@
                     cross_ref[step, at, NF:] = (lim * rre - lre * rim).astype(BF)
 
             cross = cross_ref[step]
-            probe = dot(high_ref[...], cross, NT) + dot(low_ref[...], cross, NT)
+            probe = dot(probe_ref[0], cross, NT) + dot(probe_ref[1], cross, NT)
             high, low = split(jnp.where(own_block(lanes, RANK, rows, 2 * win), probe, 0.0))
-            raw = dot(high, cross) + dot(low, cross)
-            raw_buf[k, g * lanes : (g + 1) * lanes, :] = raw.astype(BF)
+            raw_buf[k, g] = (dot(high, cross) + dot(low, cross)).astype(BF)
+            if k:
+                sent[k, g] = send(
+                    raw_buf.at[k, g], raw_in.at[k - 1, g], (rs, rr), (k - 1, g), device(k, 0)
+                )
             wide = cross.astype(F32)
             energy = jnp.sum(wide * wide, axis=1, keepdims=True)
             energy = jnp.where(own_block(rows, 2 * win, lanes, RANK), energy, 0.0)
             energy_ref[step] = jnp.sum(energy, axis=0, keepdims=True)
-        if k:
-            sent[k] = send(raw_buf.at[k], raw_in.at[k - 1], (rs, rr), k - 1, device(k, 0))
-
-    raw = raw_buf[0].astype(F32)
-    for k in order:
-        sent[k].wait()
-        raw = raw + raw_in[k - 1].astype(F32)
-    dual = full(raw, product_ref[...])
-    back = eliminate(full(raw, dual, NT))
-    dual_ref[0] = full(back, dual).astype(BF)
-    sent = {}
-    for k in order:
-        sent[k] = send(dual_ref.at[0], dual_ref.at[k], (ds, dr), k - 1, device(k, 0))
+
+    relay = chips == 4 and groups == 2
+    loads[1].wait()
+    raws, backs, given = [], [], {}
+    for g in range(groups):
+        raw = raw_buf[0, g].astype(F32)
+        for k in order:
+            sent[k, g].wait()
+            raw = raw + raw_in[k - 1, g].astype(F32)
+        high, low = split(raw)
+        dual = dot(high, product_ref[0]) + (dot(high, product_ref[1]) + dot(low, product_ref[0]))
+        back = eliminate(full(raw, dual, NT))
+        dual_ref[0, g] = full(back, dual).astype(BF)
+        for k in order:
+            if not (relay and k == 3):
+                given[k, g] = send(
+                    dual_ref.at[0, g], dual_ref.at[k, g], (ds, dr), (k - 1, g), device(k, 0)
+                )
+        raws.append(raw)
+        backs.append(back)
+
+    def add_up(k, g):
+        step = there[k] * groups + g
+        coeffs = dot(cross_ref[step], dual_ref[k, g], NT)
+        coeffs = jnp.where(own_block(rows, 2 * win, lanes, RANK), coeffs, 0.0)
+        total = jnp.sum(coeffs, axis=0, keepdims=True)
+        power = jnp.sum(coeffs * coeffs, axis=0, keepdims=True)
+        pad = jnp.zeros((5, lanes), F32)
+        sums_buf[k, g] = jnp.concatenate([total, power, energy_ref[step], pad], axis=0)
 
     summed = {}
+    if relay:
+        for g, via, to in ((0, 1, 2), (1, 2, 1)):
+            given[via, g].wait()
+            given[3, g] = send(
+                dual_ref.at[via, g], dual_ref.at[3, g], (ds, dr), (2, g), device(to, 0)
+            )
+    else:
+        for k in order:
+            for g in range(groups):
+                given[k, g].wait()
     for k in [0] + order[::-1]:
-        if k:
-            sent[k].wait()
         for g in range(groups):
-            step = there[k] * groups + g
-            part = dual_ref[k, g * lanes : (g + 1) * lanes, :]
-            coeffs = dot(cross_ref[step], part, NT)
-            coeffs = jnp.where(own_block(rows, 2 * win, lanes, RANK), coeffs, 0.0)
-            total = jnp.sum(coeffs, axis=0, keepdims=True)
-            power = jnp.sum(coeffs * coeffs, axis=0, keepdims=True)
-            pad = jnp.zeros((5, lanes), F32)
-            sums_buf[k, g] = jnp.concatenate([total, power, energy_ref[step], pad], axis=0)
+            if relay and k and (k, g) not in ((1, 0), (2, 1)):
+                given[k, g].wait()
+            add_up(k, g)
         if k:
             summed[k] = send(sums_buf.at[k], sums_in.at[k - 1], (ss, sr), k - 1, device(k, 0))
     sums = sums_buf[0]
@@ -268,45 +287,63 @@
         sums = sums + sums_in[k - 1]
     total, power, energy = sums[:, 0:1, :], sums[:, 1:2, :], sums[:, 2:3, :]
     weight = power / (power + energy / (2 * NF)) * total / windows
-    weight = jnp.concatenate([weight[g] for g in range(groups)], axis=1)
-    pairs = groups * GROUP
-    weight = jnp.where(own_block(pairs, 1, pairs * RANK, RANK), weight, 0.0)
-    out_ref[core, me] = full(full(weight, back), raw)
+    for g in range(groups):
+        spread = jnp.where(own_block(GROUP, 1, lanes, RANK), weight[g], 0.0)
+        out_ref[core, me, g * GROUP : (g + 1) * GROUP, :] = full(full(spread, backs[g]), raws[g])
     mine = out_ref.at[core, me]
     last = [send(mine, mine, (ws, wr), 2 * k + c - 1, device(k, c)) for k, c in everyone]
     for copy in last:
         copy.wait()
 
 
-def pair_weights(flat, slots, high, low, product, chips, windows):
-    parts, _, win, _ = flat.shape
+def pair_weights(records, idx, slots, sketch, held, n, chips, windows):
+    forward, inverse, product = held
+    _, win, _ = records.shape
     pairs = slots.shape[0] // 2
     groups = pairs // chips // GROUP
     lanes = GROUP * RANK
     steps = pairs // GROUP
     vmem = pl.BlockSpec(memory_space=pltpu.VMEM)
+    smem = pl.BlockSpec(memory_space=pltpu.SMEM)
+    hbm = pl.BlockSpec(memory_space=pl.ANY)
     dma = pltpu.SemaphoreType.DMA
     return pl.pallas_call(
-        functools.partial(pair_kernel, chips, windows),
-        in_specs=[pl.BlockSpec(memory_space=pltpu.SMEM)] + [vmem] * 4,
+        functools.partial(kernel, n, chips, windows),
+        in_specs=[smem, smem, vmem, vmem, vmem, hbm, hbm],
         out_specs=vmem,
         out_shape=jax.ShapeDtypeStruct((2, chips, pairs // chips, 2 * NF), F32),
         scratch_shapes=[
-            pltpu.VMEM((steps, GROUP * parts * win, 2 * NF), BF),
-            pltpu.VMEM((chips, groups * lanes, 2 * NF), BF),
-            pltpu.VMEM((chips - 1, groups * lanes, 2 * NF), BF),
+            pltpu.VMEM(inverse.shape, BF),
+            pltpu.VMEM(product.shape, BF),
+            pltpu.VMEM((n - 1, CAP, win, 2 * NF), BF),
+            pltpu.VMEM((2, n * CAP, win, 2 * NF), BF),
+            pltpu.VMEM((2, lanes, 2 * NF), BF),
+            pltpu.VMEM((steps, GROUP * 2 * win, 2 * NF), BF),
+            pltpu.VMEM((chips, groups, lanes, 2 * NF), BF),
+            pltpu.VMEM((chips - 1, groups, lanes, 2 * NF), BF),
             pltpu.VMEM((steps, 1, lanes), F32),
-            pltpu.VMEM((chips, groups * lanes, 2 * NF), BF),
+            pltpu.VMEM((chips, groups, lanes, 2 * NF), BF),
             pltpu.VMEM((chips, groups, 8, lanes), F32),
             pltpu.VMEM((chips - 1, groups, 8, lanes), F32),
-        ]
-        + [dma((chips - 1,))] * 6
-        + [dma((2 * chips - 1,))] * 2,
+            dma((2,)),
+            dma((n - 1,)),
+            dma((n - 1,)),
+            dma((n,)),
+            dma((n,)),
+            dma((chips - 1, groups)),
+            dma((chips - 1, groups)),
+            dma((chips - 1, groups)),
+            dma((chips - 1, groups)),
+            dma((chips - 1,)),
+            dma((chips - 1,)),
+            dma((2 * chips - 1,)),
+            dma((2 * chips - 1,)),
+        ],
         compiler_params=pltpu.CompilerParams(
-            vmem_limit_bytes=VMEM, collective_id=1, has_side_effects=True
+            vmem_limit_bytes=VMEM, collective_id=0, has_side_effects=True
         ),
         name="pair_weights",
-    )(slots, flat, high, low, product)
+    )(idx, slots, records, forward, sketch, inverse, product)
 
 
 def stack_kernel(weights_ref, inverse_ref, out_ref):
@@ -358,16 +395,10 @@
     ch_dev, win, _ = records.shape
     half = PAIRS_DEV // cores
     idx, slots = plan(pair_list, n_pair, ch_dev, owner)
-    flat = white_exchange(records, idx, forward)
-    flat = flat.reshape(cores, n_pair * CAP, win, 2 * NF)
-
-    probe = jnp.einsum("rl,fl->rf", sketch, inverse.astype(F32), precision=HIGHEST)
-    high = lax.reduce_precision(probe, 8, 7)
-    low = (probe - high).astype(BF)
-    high = jnp.tile(high.astype(BF), (GROUP, 1))
-    low = jnp.tile(low, (GROUP, 1))
     slots = lax.dynamic_slice_in_dim(slots, core * half * 2, half * 2, 0)
-    weights = pair_weights(flat, slots, high, low, product, chips, win * chips * cores)
+    held = (forward, inverse, product)
+    windows = win * chips * cores
+    weights = pair_weights(records, idx, slots, sketch, held, n_pair, chips, windows)
     return stack(weights.reshape(PAIRS_DEV, 2 * NF), inverse)
 
 

time: 140 us -> 111 us (0.79)
  Pallas kernels: 129 us -> 107 us
  matrix products: 5.53 us -> 0 us
  local copies, waits for them, and re-layouts: 4.14 us -> 2.73 us
    pallas_call x2 -> x1, Pallas kernels: 124 us -> 102 us  [pair_weights(): pl.pallas_call(functools.partial(kernel, n, chips, windows), in_specs=[sm...]
    dot_general x1 -> x0, matrix products: 5.53 us -> none  [local(): jnp.einsum('rl,fl->rf', sketch, inverse.astype(F32), precision=HIGHEST)]
    another operation x2 -> x0, local copies, waits for them, and re-layouts: 1.46 us -> none  [the longest x1 0.73 us: local(): low = jnp.tile(low, (GROUP, 1))]
where the time goes in v3:
time: 111 us
  Pallas kernels  107 us (96%)
  local copies, waits for them, and re-layouts  2.73 us (2%)
    pallas_call x1, Pallas kernels, pair_weights(): pl.pallas_call(functools.partial(kernel, n, chips, windows), in_specs=[sm...  102 us
    pallas_call x1, Pallas kernels, stack(): pl.pallas_call(stack_kernel, grid=(LAGS // tile,), in_specs=[pl.BlockSpec...  5 us

profile of v3, /device:TPU:9, one launch (start us, length us, event | category | flops | bytes accessed | tf_op | source)
XLA Modules:
  0.0 110.7 jit_solution(15430518957532462415)
XLA Ops:
  0.0 0.1 add.23
  0.1 0.1 add.24
  0.2 0.8 copy.10
  1.0 0.2 eq.45
  1.2 0.2 fusion
  1.4 0.1 reshape.33
  1.5 0.4 convert_reduce_fusion
  1.9 0.1 reduce_sum.31
  2.0 0.2 select_reduce_fusion
  2.2 0.7 dynamic_slice.19.slot_ref
  2.9 0.3 select_reduce_fusion.1
  3.1 0.1 copy.11
  3.2 0.6 reshape.34.idx_ref
  3.8 101.8 %pair_weights.1 = f32[2,4,16,1024]{3,2,1,0:T(8,128)} custom-call(s32[48]{0:T(128)} %reshape.34.idx_ref, s32[128]{0:T(128)} %dynamic_slice.19.slot_ref, bf16[64,16,2048]{2,1,0:T(8,128)(2,1)} %records_ref.1, bf16[2048,1024]{1,0:T(8,128)(2,1)} %constant.29.clone.forward_ref, f32[16,2048]{1,0:T(8,128)} %sketch_ref.1, ...), custom_call_target="tpu_custom_call" | custom-call | tf_op jit(solution)/shard_map/pair_weights/pallas_call | solution.py:310
  105.7 5.0 %stack.1 = f32[128,2048]{1,0:T(8,128)} custom-call(f32[128,1024]{1,0:T(8,128)} %bitcast.7, bf16[1024,2048]{1,0:T(8,128)(2,1)} %constant.30.clone.inverse_hbm.inverse_ref), custom_call_target="tpu_custom_call" | custom-call | tf_op jit(solution)/shard_map/stack/pallas_call | solution.py:357
  (6 shorter events, 0.1 us)

commit v4 on v3

--- a/solution.py
+++ b/solution.py
@@ -124,8 +124,8 @@
 
 
 def kernel(
-    n, chips, windows, idx_ref, slot_ref, records_ref, forward_ref, sketch_ref, inverse_hbm,
-    product_hbm, out_ref, inverse_ref, product_ref, white_buf, flat_ref, probe_ref, cross_ref,
+    n, chips, windows, idx_ref, slot_ref, sketch_ref, records_hbm, forward_hbm, inverse_hbm,
+    product_hbm, out_ref, records_ref, forward_ref, inverse_ref, product_ref, share_ref, white_buf, flat_ref, probe_ref, cross_ref,
     raw_buf, raw_in, energy_ref, dual_ref, sums_buf, sums_in,
     load, zs, zr, cs, cr, rs, rr, ds, dr, ss, sr, ws, wr,
 ):
@@ -143,14 +143,19 @@
         return {"chip": there[k], "core": 1 - core if c else core}
 
     loads = [
-        pltpu.make_async_copy(inverse_hbm, inverse_ref, load.at[0]),
-        pltpu.make_async_copy(product_hbm, product_ref, load.at[1]),
+        pltpu.make_async_copy(forward_hbm, forward_ref, load.at[0]),
+        pltpu.make_async_copy(records_hbm, records_ref, load.at[1]),
+        pltpu.make_async_copy(inverse_hbm, inverse_ref, load.at[2]),
+        pltpu.make_async_copy(product_hbm, product_ref, load.at[3]),
     ]
     for copy in loads:
         copy.start()
     greet(
         [{"pair": partner(owner, k, n)} for k in range(1, n)] + [device(k, c) for k, c in everyone]
     )
+
+    loads[0].wait()
+    loads[1].wait()
 
     def slots_of(o):
         return pl.ds(pl.multiple_of(o * CAP, CAP), CAP)
@@ -185,7 +190,7 @@
     block = flat_ref.at[core, slots_of(owner)]
     shared = [send(block, block, (cs, cr), 0, device(0, 1))]
 
-    loads[0].wait()
+    loads[2].wait()
     first = sketch_ref[...].astype(BF)
     second, third = split(sketch_ref[...] - first.astype(F32))
     probes = dot(jnp.concatenate([first, second, third], axis=0), inverse_ref[...], NT)
@@ -235,7 +240,7 @@
             energy_ref[step] = jnp.sum(energy, axis=0, keepdims=True)
 
     relay = chips == 4 and groups == 2
-    loads[1].wait()
+    loads[3].wait()
     raws, backs, given = [], [], {}
     for g in range(groups):
         raw = raw_buf[0, g].astype(F32)
@@ -287,34 +292,46 @@
         sums = sums + sums_in[k - 1]
     total, power, energy = sums[:, 0:1, :], sums[:, 1:2, :], sums[:, 2:3, :]
     weight = power / (power + energy / (2 * NF)) * total / windows
+    mixed = []
     for g in range(groups):
         spread = jnp.where(own_block(GROUP, 1, lanes, RANK), weight[g], 0.0)
-        out_ref[core, me, g * GROUP : (g + 1) * GROUP, :] = full(full(spread, backs[g]), raws[g])
-    mine = out_ref.at[core, me]
+        mixed.append(full(full(spread, backs[g]), raws[g]))
+    share_ref[core, me] = jnp.concatenate(mixed, axis=0).astype(share_ref.dtype)
+    mine = share_ref.at[core, me]
     last = [send(mine, mine, (ws, wr), 2 * k + c - 1, device(k, c)) for k, c in everyone]
     for copy in last:
         copy.wait()
 
-
-def pair_weights(records, idx, slots, sketch, held, n, chips, windows):
+    weights = share_ref[...].reshape(PAIRS_DEV, 2 * NF)
+    terms = [weights] if weights.dtype == BF else split(weights)
+    for at in range(0, LAGS, 512):
+        tile = inverse_ref[:, at : at + 512]
+        out_ref[:, at : at + 512] = sum(dot(term, tile) for term in terms)
+
+
+def pair_stacks(records, idx, slots, sketch, held, n, chips, windows):
     forward, inverse, product = held
     _, win, _ = records.shape
     pairs = slots.shape[0] // 2
     groups = pairs // chips // GROUP
     lanes = GROUP * RANK
     steps = pairs // GROUP
+    own = pairs // chips
     vmem = pl.BlockSpec(memory_space=pltpu.VMEM)
     smem = pl.BlockSpec(memory_space=pltpu.SMEM)
     hbm = pl.BlockSpec(memory_space=pl.ANY)
     dma = pltpu.SemaphoreType.DMA
     return pl.pallas_call(
         functools.partial(kernel, n, chips, windows),
-        in_specs=[smem, smem, vmem, vmem, vmem, hbm, hbm],
+        in_specs=[smem, smem, vmem, hbm, hbm, hbm, hbm],
         out_specs=vmem,
-        out_shape=jax.ShapeDtypeStruct((2, chips, pairs // chips, 2 * NF), F32),
+        out_shape=jax.ShapeDtypeStruct((2 * pairs, LAGS), F32),
         scratch_shapes=[
+            pltpu.VMEM(records.shape, BF),
+            pltpu.VMEM(forward.shape, BF),
             pltpu.VMEM(inverse.shape, BF),
             pltpu.VMEM(product.shape, BF),
+            pltpu.VMEM((2, chips, own, 2 * NF), BF if own % 16 == 0 else F32),
             pltpu.VMEM((n - 1, CAP, win, 2 * NF), BF),
             pltpu.VMEM((2, n * CAP, win, 2 * NF), BF),
             pltpu.VMEM((2, lanes, 2 * NF), BF),
@@ -325,7 +342,7 @@
             pltpu.VMEM((chips, groups, lanes, 2 * NF), BF),
             pltpu.VMEM((chips, groups, 8, lanes), F32),
             pltpu.VMEM((chips - 1, groups, 8, lanes), F32),
-            dma((2,)),
+            dma((4,)),
             dma((n - 1,)),
             dma((n - 1,)),
             dma((n,)),
@@ -342,30 +359,8 @@
         compiler_params=pltpu.CompilerParams(
             vmem_limit_bytes=VMEM, collective_id=0, has_side_effects=True
         ),
-        name="pair_weights",
-    )(idx, slots, records, forward, sketch, inverse, product)
-
-
-def stack_kernel(weights_ref, inverse_ref, out_ref):
-    high, low = split(weights_ref[...])
-    out_ref[...] = dot(high, inverse_ref[...]) + dot(low, inverse_ref[...])
-
-
-def stack(weights, inverse):
-    pairs = weights.shape[0]
-    tile = 512
-    return pl.pallas_call(
-        stack_kernel,
-        grid=(LAGS // tile,),
-        in_specs=[
-            pl.BlockSpec(weights.shape, lambda i: (0, 0)),
-            pl.BlockSpec((2 * NF, tile), lambda i: (0, i)),
-        ],
-        out_specs=pl.BlockSpec((pairs, tile), lambda i: (0, i)),
-        out_shape=jax.ShapeDtypeStruct((pairs, LAGS), F32),
-        compiler_params=params(),
-        name="stack",
-    )(weights, inverse)
+        name="pair_stacks",
+    )(idx, slots, sketch, records, forward, inverse, product)
 
 
 def plan(pair_list, n_pair, ch_dev, owner):
@@ -398,8 +393,7 @@
     slots = lax.dynamic_slice_in_dim(slots, core * half * 2, half * 2, 0)
     held = (forward, inverse, product)
     windows = win * chips * cores
-    weights = pair_weights(records, idx, slots, sketch, held, n_pair, chips, windows)
-    return stack(weights.reshape(PAIRS_DEV, 2 * NF), inverse)
+    return pair_stacks(records, idx, slots, sketch, held, n_pair, chips, windows)
 
 
 def solution(mesh):

time: 111 us -> 106 us (0.955)
  Pallas kernels: 107 us -> 98.9 us
  local copies, waits for them, and re-layouts: 2.73 us -> 5.02 us
    pallas_call x2 -> x1, Pallas kernels: 107 us -> 98.9 us  [pair_stacks(): pl.pallas_call(functools.partial(kernel, n, chips, windows), in_specs=[sm...]
    unnamed x2 -> x3, local copies, waits for them, and re-layouts: 0.83 us -> 3.13 us
where the time goes in v4:
time: 106 us; the launch traced here: 105 us
  Pallas kernels  98.9 us (93%)
  local copies, waits for them, and re-layouts  5.02 us (5%)
  other arithmetic  1.07 us (1%)
    pallas_call x1, Pallas kernels, pair_stacks(): pl.pallas_call(functools.partial(kernel, n, chips, windows), in_specs=[sm...  98.9 us
    unnamed x3, local copies, waits for them, and re-layouts  3.13 us

profile of v4, /device:TPU:9, one launch (start us, length us, event | category | flops | bytes accessed | tf_op | source)
XLA Modules:
  0.0 105.1 jit_solution(12734217503468878895)
XLA Ops:
  0.0 0.1 add.23
  0.1 0.1 add.24
  0.2 0.8 copy.10
  1.0 0.2 eq.45
  1.2 0.2 fusion
  1.4 0.1 reshape.30
  1.5 0.4 convert_reduce_fusion
  1.9 0.1 reduce_sum.31
  2.0 0.2 select_reduce_fusion
  2.2 0.7 dynamic_slice.19.slot_ref
  2.9 0.3 select_reduce_fusion.1
  3.1 0.1 copy.11
  3.2 0.6 reshape.31.idx_ref
  3.8 98.9 %pair_stacks.1 = f32[128,2048]{1,0:T(8,128)} custom-call(s32[48]{0:T(128)} %reshape.31.idx_ref, s32[128]{0:T(128)} %dynamic_slice.19.slot_ref, f32[16,2048]{1,0:T(8,128)} %sketch_ref.1, bf16[64,16,2048]{2,1,0:T(8,128)(2,1)} %records_hbm.1, bf16[2048,1024]{1,0:T(8,128)(2,1)} %constant.29.clone.forward_hbm, bf16[1024,2048]{1,0:T(8,128)(2,1)} %constant.30.clone.inverse_hbm, ...), custom_call_target="tpu_custom_call" | custom-call | tf_op jit(solution)/shard_map/pair_stacks/pallas_call | solution.py:324
  102.8 2.3 %copy.16 = f32[128,2048]{1,0:T(8,128)} copy(f32[128,2048]{1,0:T(8,128)} %pair_stacks.1) | data formatting | bytes 2097152
  (6 shorter events, 0.1 us)

commit v5 on v4

--- a/solution.py
+++ b/solution.py
@@ -137,6 +137,7 @@
     lanes = GROUP * RANK
     win = records_ref.shape[1]
     rows = GROUP * 2 * win
+    first_pair = core * (slot_ref.shape[0] // 4)
     everyone = [(k, c) for k in range(chips) for c in range(2) if k or c]
 
     def device(k, c):
@@ -161,7 +162,7 @@
         return pl.ds(pl.multiple_of(o * CAP, CAP), CAP)
 
     def whitened(d, put):
-        block = jnp.concatenate([records_ref[idx_ref[d * CAP + j]] for j in range(CAP)], axis=0)
+        block = jnp.concatenate([records_ref[idx_ref[d, j]] for j in range(CAP)], axis=0)
         spectra = dot(block, forward_ref[...])
         re, im = spectra[:, :NF], spectra[:, NF:]
         power = re * re + im * im
@@ -215,8 +216,8 @@
 
             @pl.loop(0, GROUP)
             def _(q, step=step):
-                a = slot_ref[(step * GROUP + q) * 2]
-                b = slot_ref[(step * GROUP + q) * 2 + 1]
+                a = slot_ref[(first_pair + step * GROUP + q) * 2]
+                b = slot_ref[(first_pair + step * GROUP + q) * 2 + 1]
                 for part in range(2):
                     left = flat_ref[part, a].astype(F32)
                     right = flat_ref[part, b].astype(F32)
@@ -312,7 +313,7 @@
 def pair_stacks(records, idx, slots, sketch, held, n, chips, windows):
     forward, inverse, product = held
     _, win, _ = records.shape
-    pairs = slots.shape[0] // 2
+    pairs = slots.shape[0] // 4
     groups = pairs // chips // GROUP
     lanes = GROUP * RANK
     steps = pairs // GROUP
@@ -373,7 +374,7 @@
     mine = lax.dynamic_slice_in_dim(blocks, owner, 1, 1)[:, 0]
     mine_rank = lax.dynamic_slice_in_dim(rank, owner, 1, 1)[:, 0]
     hit = mine[:, None, :] & (mine_rank[:, None, :] == jnp.arange(CAP)[None, :, None])
-    idx = jnp.sum(jnp.where(hit, jnp.arange(ch_dev), 0), axis=2).reshape(-1)
+    idx = jnp.sum(jnp.where(hit, jnp.arange(ch_dev), 0), axis=2)
     place = (rank + CAP * jnp.arange(n_pair)[None, :, None]).reshape(n_pair, -1)
     place = lax.dynamic_slice_in_dim(place, owner, 1, 0)[0]
     wanted = lax.dynamic_slice_in_dim(lists, owner, 1, 0)[0]
@@ -386,11 +387,8 @@
     chips = lax.axis_size("chip")
     cores = lax.axis_size("core")
     owner = lax.axis_index("pair")
-    core = lax.axis_index("core")
     ch_dev, win, _ = records.shape
-    half = PAIRS_DEV // cores
     idx, slots = plan(pair_list, n_pair, ch_dev, owner)
-    slots = lax.dynamic_slice_in_dim(slots, core * half * 2, half * 2, 0)
     held = (forward, inverse, product)
     windows = win * chips * cores
     return pair_stacks(records, idx, slots, sketch, held, n_pair, chips, windows)

time: 106 us -> 106 us (level)
  no operation moved by 1% of the time
where the time goes in v5:
time: 106 us; the launch traced here: 105 us
  Pallas kernels  99 us (93%)
  local copies, waits for them, and re-layouts  4.32 us (4%)
  other arithmetic  1.67 us (2%)
    pallas_call x1, Pallas kernels, pair_stacks(): pl.pallas_call(functools.partial(kernel, n, chips, windows), in_specs=[sm...  99 us
    unnamed x3, local copies, waits for them, and re-layouts  3.13 us

profile of v5, /device:TPU:9, one launch (start us, length us, event | category | flops | bytes accessed | tf_op | source)
XLA Modules:
  0.0 105.0 jit_solution(9079252055357873745)
XLA Ops:
  0.0 0.1 add.20
  0.1 0.1 add.21
  0.2 0.8 copy.10
  1.0 0.2 eq.45
  1.2 0.2 fusion
  1.4 0.1 reshape.27
  1.5 0.4 convert_reduce_fusion
  1.9 0.1 reduce_sum.31
  2.0 0.8 select_reduce_fusion.slot_ref
  2.8 0.3 select_reduce_fusion.1
  3.1 0.7 copy.11.idx_ref
  3.7 99.0 %pair_stacks.1 = f32[128,2048]{1,0:T(8,128)} custom-call(s32[4,12]{1,0:T(4,128)} %copy.11.idx_ref, s32[256]{0:T(256)} %select_reduce_fusion.slot_ref, f32[16,2048]{1,0:T(8,128)} %sketch_ref.1, bf16[64,16,2048]{2,1,0:T(8,128)(2,1)} %records_hbm.1, bf16[2048,1024]{1,0:T(8,128)(2,1)} %constant.19.clone.forward_hbm, ...), custom_call_target="tpu_custom_call" | custom-call | tf_op jit(solution)/shard_map/pair_stacks/pallas_call | solution.py:325
  102.7 2.3 %copy.16 = f32[128,2048]{1,0:T(8,128)} copy(f32[128,2048]{1,0:T(8,128)} %pair_stacks.1) | data formatting | bytes 2097152
  (6 shorter events, 0.1 us)
